TPU v7x, 512 devices: a whole 4x4x16 slice. The times are simulated.
512 devices in a mesh: gx: 32 (over z, x_hi), gy: 16 (over y, x_lo, core).
Axes of the slice: x: 4 (x_hi: 2, x_lo: 2; x = x_hi * 2 + x_lo), y: 4, z: 16, core: 2. Of those that a mesh axis runs over, the one named last changes fastest.
Arguments:
- flow_field: bfloat16 [1024, 512, 2048], P('gx', 'gy'), may hold values from -6 to 6
- y_factor: bfloat16 [512, 128], P('gy'), may hold values from -0.25 to 0.25
- z_factor: bfloat16 [64, 16], replicated, may hold values from -0.75 to 0.75
- v_factor: bfloat16 [32, 8], replicated, may hold values from -1 to 1
- x_start: float32 [1024, 128], P('gx'), may hold values from -0.1875 to 0.1875
Outputs:
- x_factor: float32 [1024, 128], P('gx')
- core_tensor: float32 [128, 16384], P('gx', 'gy')
All inputs are finite; a program needn't handle non-finite values.
Results may differ from a plain program's by a relative error of at most 0.0051.
Values sent between devices are 32-bit elements; how exact they have to be, the bound alone decides.
No kernel may reach another device: no remote copies, remote signals or barrier semaphores. Data moves between devices by JAX's collectives and lax.ppermute only.
A program may use at most 64 MiB of HBM per device.

v0:
```python
import jax
import jax.numpy as jnp
from jax import lax
from jax.sharding import PartitionSpec as P

NZ = 64
NV = 32
RY = 128
RZ = 16
RV = 8
ITERS = 3


def kronecker_table(z_factor, v_factor):
    table = (
        z_factor.astype(jnp.float32)[:, None, :, None]
        * v_factor.astype(jnp.float32)[None, :, None, :]
    )
    return table.reshape(NZ * NV, RZ * RV).astype(jnp.bfloat16)


def orthonormal(image_rows):
    local_correlation = lax.dot_general(
        image_rows, image_rows, (((0,), (0,)), ((), ())), precision=lax.Precision.HIGHEST
    )
    correlation = lax.psum(local_correlation, "gx")
    lower_factor = jnp.linalg.cholesky(correlation)
    return lax.linalg.triangular_solve(
        lower_factor, image_rows, left_side=False, lower=True, transpose_a=True
    )


def local(flow_field, y_factor, z_factor, v_factor, x_start):
    rows_here = flow_field.shape[0]
    cols_here = flow_field.shape[1]
    kronecker = kronecker_table(z_factor, v_factor)
    reduced = jnp.dot(
        flow_field.reshape(rows_here * cols_here, NZ * NV),
        kronecker,
        preferred_element_type=jnp.float32,
    )
    reduced = reduced.astype(jnp.bfloat16).reshape(rows_here, cols_here, RZ * RV)
    partial_rows = jnp.einsum("ayk,yq->aqk", reduced, y_factor, preferred_element_type=jnp.float32)
    partial_rows = partial_rows.reshape(rows_here, RY * RZ * RV)
    core_cols = RY * RZ * RV // lax.axis_size("gy")
    summed = lax.psum(partial_rows, "gy")
    projected = lax.dynamic_slice_in_dim(summed, lax.axis_index("gy") * core_cols, core_cols, 1)
    basis_now = x_start
    for sweep in range(ITERS):
        local_left = lax.dot_general(
            projected, basis_now, (((0,), (0,)), ((), ())), precision=lax.Precision.HIGHEST
        )
        left_side = lax.psum(local_left, "gx")
        local_image = jnp.dot(projected, left_side, precision=lax.Precision.HIGHEST)
        image_rows = lax.psum(local_image, "gy")
        basis_now = orthonormal(image_rows)
    core_tensor = lax.psum_scatter(
        lax.dot_general(
            basis_now, projected, (((0,), (0,)), ((), ())), precision=lax.Precision.HIGHEST
        ),
        "gx",
        scatter_dimension=0,
        tiled=True,
    )
    return (basis_now, core_tensor)


def solution(mesh):
    placed = (P("gx", "gy", None), P("gy", None), P(), P(), P("gx", None))
    return jax.shard_map(
        local, mesh=mesh, in_specs=placed, out_specs=(P("gx", None), P("gx", "gy")), check_vma=False
    )
```

profile of v0, /device:TPU:1, one launch (start us, length us, event | category | flops | bytes accessed | tf_op | source)
XLA Modules:
  0.0 2471.0 jit_solution(17271367850174509234)
XLA Ops:
  7.2 0.0 all-reduce.10.cloned.1.call-start
  7.2 0.7 convert_element_type.25
  7.9 0.7 convert_element_type.24
  8.6 0.6 multiply_convert_fusion
  9.2 2.3 convert_element_type.27
  11.5 3.7 fusion
  15.2 0.2 copy.24
  15.4 0.5 convolution_bitcast_fusion
  15.8 1.9 copy.25
  17.7 4.1 copy.37
  21.9 0.0 all-reduce.12.cloned.1.call-start
  21.9 145.6 %all-reduce.10.cloned.1.call-done = f32[32,16384]{1,0:T(8,128)} async-done(((f32[32,16384]{1,0:T(8,128)}), f32[32,16384]{1,0:T(8,128)}) %all-reduce.10.cloned.1.call-update) | async-done | bytes 2097168 | tf_op jit(solution)/shard_map/psum | solution.py:46
  167.5 2.7 fusion.13
  170.2 0.0 all-reduce.12.cloned.1.call-update
  170.3 0.0 all-reduce.14.cloned.1.call-start
  170.3 287.1 %all-reduce.12.cloned.1.call-done = f32[1024,128]{1,0:T(8,128)} async-done(((f32[1024,128]{1,0:T(8,128)}), f32[1024,128]{1,0:T(8,128)}) %all-reduce.12.cloned.1.call-update) | async-done | bytes 524304 | tf_op jit(solution)/shard_map/psum | solution.py:53
  457.4 1.5 fusion.11
  458.9 70.8 %psum.72 = f32[32,128]{1,0:T(8,128)S(1)} all-reduce(f32[32,128]{1,0:T(8,128)S(1)} %fusion.11), channel_id=1, replica_groups=mesh['gx'=32,'gy'=16] {'gy'}, use_global_device_ids=true, to_apply=%region_2.0 | all-reduce | flops 4096 | bytes 32768 | tf_op jit(solution)/shard_map/psum | solution.py:55
  529.7 0.9 fusion.36
  530.6 0.0 all-reduce.14.cloned.1.call-update
  530.6 0.2 all-reduce.16.cloned.1.call-start
  530.9 267.6 %all-reduce.14.cloned.1.call-done = f32[128,128]{0,1:T(8,128)} async-done(((f32[128,128]{0,1:T(8,128)}), f32[128,128]{0,1:T(8,128)}) %all-reduce.14.cloned.1.call-update) | async-done | bytes 65552 | tf_op jit(solution)/shard_map/psum | solution.py:26
  798.5 0.9 copy.27
  799.4 0.9 fusion.23
  800.3 11.7 cholesky.59
  812.0 0.6 compare_reduce_fusion.2
  812.7 0.7 fusion.15
  813.4 9.8 custom-call.7
  823.2 0.2 convolution_bitcast_fusion.3
  823.3 2.7 fusion.9
  826.1 0.0 all-reduce.16.cloned.1.call-update
  826.1 0.0 all-reduce.18.cloned.1.call-start
  826.1 299.8 %all-reduce.16.cloned.1.call-done = f32[1024,128]{1,0:T(8,128)} async-done(((f32[1024,128]{1,0:T(8,128)}), f32[1024,128]{1,0:T(8,128)}) %all-reduce.16.cloned.1.call-update) | async-done | bytes 524304 | tf_op jit(solution)/shard_map/psum | solution.py:53
  1126.0 1.5 fusion.7
  1127.5 70.8 %psum.75 = f32[32,128]{1,0:T(8,128)S(1)} all-reduce(f32[32,128]{1,0:T(8,128)S(1)} %fusion.7), channel_id=1, replica_groups=mesh['gx'=32,'gy'=16] {'gy'}, use_global_device_ids=true, to_apply=%region_7.10 | all-reduce | flops 4096 | bytes 32768 | tf_op jit(solution)/shard_map/psum | solution.py:55
  1198.3 0.9 fusion.37
  1199.2 0.3 all-reduce.20.cloned.1.call-start
  1199.5 267.6 %all-reduce.18.cloned.1.call-done = f32[128,128]{0,1:T(8,128)} async-done(((f32[128,128]{0,1:T(8,128)}), f32[128,128]{0,1:T(8,128)}) %all-reduce.18.cloned.1.call-update) | async-done | bytes 65552 | tf_op jit(solution)/shard_map/psum | solution.py:26
  1467.1 0.9 copy.29
  1468.1 0.9 fusion.21
  1468.9 11.7 cholesky.70
  1480.7 0.6 compare_reduce_fusion.1
  1481.3 0.7 fusion.16
  1482.0 9.8 custom-call.8
  1491.8 0.2 convolution_bitcast_fusion.2
  1491.9 2.7 fusion.5
  1494.7 0.0 all-reduce.22.cloned.1.call-start
  1494.7 299.8 %all-reduce.20.cloned.1.call-done = f32[1024,128]{1,0:T(8,128)} async-done(((f32[1024,128]{1,0:T(8,128)}), f32[1024,128]{1,0:T(8,128)}) %all-reduce.20.cloned.1.call-update) | async-done | bytes 524304 | tf_op jit(solution)/shard_map/psum | solution.py:53
  1794.6 1.5 fusion.3
  1796.1 70.8 %psum.78 = f32[32,128]{1,0:T(8,128)S(1)} all-reduce(f32[32,128]{1,0:T(8,128)S(1)} %fusion.3), channel_id=1, replica_groups=mesh['gx'=32,'gy'=16] {'gy'}, use_global_device_ids=true, to_apply=%region_10.13 | all-reduce | flops 4096 | bytes 32768 | tf_op jit(solution)/shard_map/psum | solution.py:55
  1866.9 0.9 fusion.38
  1867.9 0.3 all-reduce.24.cloned.1.call-start
  1868.2 267.6 %all-reduce.22.cloned.1.call-done = f32[128,128]{0,1:T(8,128)} async-done(((f32[128,128]{0,1:T(8,128)}), f32[128,128]{0,1:T(8,128)}) %all-reduce.22.cloned.1.call-update) | async-done | bytes 65552 | tf_op jit(solution)/shard_map/psum | solution.py:26
  2135.7 0.9 copy.31
  2136.7 0.9 fusion.19
  2137.5 11.7 cholesky.81
  2149.3 0.6 compare_reduce_fusion
  2149.9 0.7 fusion.17
  2150.6 9.8 custom-call.9
  2160.4 0.2 convolution_bitcast_fusion.1
  2160.6 2.3 fusion.1
  2162.9 1.3 dynamic-slice
  2164.9 298.0 %all-reduce.24.cloned.1.call-done = f32[128,1024]{1,0:T(8,128)} async-done(((f32[128,1024]{1,0:T(8,128)}), f32[128,1024]{1,0:T(8,128)}) %all-reduce.24.cloned.1.call-update) | async-done | bytes 524304
  2462.8 1.4 constant_dynamic-slice_fusion
  (14 shorter events, 0.2 us)
Async XLA Ops:
  7.2 160.4 %copy-start = (f32[32,128]{1,0:T(8,128)S(1)}, f32[32,128]{1,0:T(8,128)}, u32[]{:S(2)}) copy-start(f32[32,128]{1,0:T(8,128)} %param.12) | copy-start | bytes 49156
  7.2 160.3 %all-reduce.10.cloned.1.call-start = ((), (), s32[]{:S(2)}) async-start(), calls=%async_computation | async-start | bytes 4194304 | tf_op jit(solution)/shard_map/psum | solution.py:46
  11.5 3.9 copy-start.2
  21.9 435.5 %all-reduce.12.cloned.1.call-start = ((), (), s32[]{:S(2)}) async-start(), calls=%async_computation.1 | async-start | bytes 1048576 | tf_op jit(solution)/shard_map/psum | solution.py:53
  170.3 628.2 %all-reduce.14.cloned.1.call-start = ((), (), s32[]{:S(2)}) async-start(), calls=%async_computation.2 | async-start | bytes 131072 | tf_op jit(solution)/shard_map/psum | solution.py:26
  530.6 595.3 %all-reduce.16.cloned.1.call-start = ((), (), s32[]{:S(2)}) async-start(), calls=%async_computation.3 | async-start | bytes 1048576 | tf_op jit(solution)/shard_map/psum | solution.py:53
  826.1 641.0 %all-reduce.18.cloned.1.call-start = ((), (), s32[]{:S(2)}) async-start(), calls=%async_computation.4 | async-start | bytes 131072 | tf_op jit(solution)/shard_map/psum | solution.py:26
  1199.2 595.3 %all-reduce.20.cloned.1.call-start = ((), (), s32[]{:S(2)}) async-start(), calls=%async_computation.5 | async-start | bytes 1048576 | tf_op jit(solution)/shard_map/psum | solution.py:53
  1494.7 641.0 %all-reduce.22.cloned.1.call-start = ((), (), s32[]{:S(2)}) async-start(), calls=%async_computation.6 | async-start | bytes 131072 | tf_op jit(solution)/shard_map/psum | solution.py:26
  1867.9 595.0 %all-reduce.24.cloned.1.call-start = ((), (), s32[]{:S(2)}) async-start(), calls=%async_computation.7 | async-start | bytes 1048576
  2160.6 303.6 %copy-start.1 = (f32[32,128]{1,0:T(8,128)}, f32[32,128]{1,0:T(8,128)S(1)}, u32[]{:S(2)}) copy-start(f32[32,128]{1,0:T(8,128)S(1)} %convolution_bitcast_fusion.1) | copy-start | bytes 49156
Sparse Core Ops, SparseCore 0:
  22.0 145.5 all-reduce.9
  170.4 286.8 all-reduce.11
  530.8 267.7 all-reduce.13
  826.2 299.7 all-reduce.15
  1199.4 267.7 all-reduce.17
  1494.8 299.7 all-reduce.19
  1868.0 267.7 all-reduce.21
  2163.1 299.7 all-reduce.23
where the time goes:
time: 2490 us; the launch traced here: 2470 us
  waiting for transfers between devices  2130 us (86%)
  blocking collectives  212 us (9%)
  other arithmetic  73.1 us (3%)
    psum x3, waiting for transfers between devices, local(): left_side = lax.psum(local_left, 'gx')  887 us
    psum x3, waiting for transfers between devices, orthonormal(): correlation = lax.psum(local_correlation, 'gx')  803 us
    unnamed x9, waiting for transfers between devices  298 us
    psum x3, blocking collectives, local(): image_rows = lax.psum(local_image, 'gy')  212 us
    psum x1, waiting for transfers between devices, local(): summed = lax.psum(partial_rows, 'gy')  146 us
  transfers between devices with their start and end apart: 8, of which 8 were waited for; matrix products, arithmetic and copies ran while one was open for 0% of the time, Pallas kernels for 0%

commit v1 on v0

v1 whole, which is shorter than its diff:
```python
import jax
import jax.numpy as jnp
from jax import lax
from jax.sharding import Mesh, PartitionSpec as P

NZ = 64
NV = 32
RX = 128
RY = 128
RZ = 16
RV = 8
ITERS = 3
HIGHEST = lax.Precision.HIGHEST
PLANE = ("h", "y", "l", "c")
XY = ("h", "y", "l")


def kronecker_table(z_factor, v_factor):
    table = (
        z_factor.astype(jnp.float32)[:, None, :, None]
        * v_factor.astype(jnp.float32)[None, :, None, :]
    )
    return table.reshape(NZ * NV, RZ * RV).astype(jnp.bfloat16)


def gather_by_exchange(block, axes):
    count = lax.axis_size(axes)
    return lax.all_to_all(jnp.broadcast_to(block[None], (count, *block.shape)), axes, 0, 0)


def orthonormal(image_rows):
    correlation = lax.dot_general(
        image_rows, image_rows, (((0,), (0,)), ((), ())), precision=HIGHEST
    )
    lower_factor = jnp.linalg.cholesky(correlation)
    return lax.linalg.triangular_solve(
        lower_factor, image_rows, left_side=False, lower=True, transpose_a=True
    )


def local(flow_field, y_factor, z_factor, v_factor, x_start):
    z = lax.axis_index("z")
    h = lax.axis_index("h")
    kronecker = kronecker_table(z_factor, v_factor)
    reduced = lax.dot_general(
        kronecker,
        flow_field.reshape(1024, NZ * NV),
        (((0,), (1,)), ((), ())),
        preferred_element_type=jnp.float32,
    )
    reduced = lax.reduce_precision(reduced, 8, 7)
    y_half = lax.dynamic_slice_in_dim(y_factor, h * 16, 16, 0).astype(jnp.float32)
    send = jnp.concatenate(
        [reduced.reshape(32, 32, 128), jnp.broadcast_to(y_half[None], (32, 16, 128))], axis=1
    )
    got = lax.all_to_all(send, PLANE, 0, 0).reshape(2, 16, 48, 128)
    table = got[:, :, 32:, :].transpose(1, 0, 2, 3).reshape(16, 32, 128)
    rows = got[:, :, :32, :].reshape(2, 16, 4, 8, 4, 32)
    projected = jnp.einsum(
        "hgkjay,gyq->hjakq", rows, table, precision=HIGHEST
    ).reshape(64, 512)
    start = gather_by_exchange(x_start, "h").reshape(64, RX)
    basis = lax.all_gather(start, "z").reshape(1024, RX)
    every = lax.all_gather(projected, "z").reshape(1024, 512)
    gram = lax.dot_general(every, every, (((1,), (1,)), ((), ())), precision=HIGHEST)
    gram = lax.all_to_all(gram.reshape(2, 512, 1024), "c", 0, 0).sum(0)
    gram = lax.all_to_all(gram.reshape(16, 32, 1024), XY, 0, 0).sum(0)
    gram = gather_by_exchange(gram, XY).reshape(512, 1024)
    gram = gather_by_exchange(gram, "c").reshape(1024, 1024)
    for sweep in range(ITERS):
        basis = orthonormal(jnp.dot(gram, basis, precision=HIGHEST))
    x_factor = lax.dynamic_slice_in_dim(basis, (z * 2 + h) * 32, 32, 0)
    mine = lax.dynamic_slice_in_dim(basis, z * 8, 8, 1)
    core = lax.dot_general(mine, every, (((0,), (0,)), ((), ())), precision=HIGHEST)
    core = core.reshape(2, 4, 4, 16, 8).transpose(0, 3, 1, 2, 4).reshape(32, 1, 128)
    core = lax.all_to_all(core, PLANE, 0, 0).reshape(32, 4, 4, 8)
    core = core.transpose(1, 3, 0, 2).reshape(4, 1024)
    return (x_factor, core)


def solution(mesh):
    fine = Mesh(mesh.devices.reshape(16, 2, 4, 2, 2), ("z", "h", "y", "l", "c"))
    gx, gy = ("z", "h"), ("y", "l", "c")
    placed = (P(gx, gy, None), P(gy, None), P(), P(), P(gx, None))
    return jax.shard_map(
        local, mesh=fine, in_specs=placed, out_specs=(P(gx, None), P(gx, gy)), check_vma=False
    )
```

time: 2490 us -> 355 us (0.14)
  waiting for transfers between devices: 2130 us -> 72.5 us
  blocking collectives: 212 us -> 117 us
    psum x7 -> x0, waiting for transfers between devices: 1840 us -> none  [the longest x3 887 us: local(): left_side = lax.psum(local_left, 'gx')]
    unnamed x9 -> x1, waiting for transfers between devices: 298 us -> 0.02 us
    psum x3 -> x0, blocking collectives: 212 us -> none  [local(): image_rows = lax.psum(local_image, 'gy')]
    all_to_all x0 -> x4, blocking collectives: none -> 89.5 us  [the longest x1 34 us: local(): gram = lax.all_to_all(gram.reshape(16, 32, 1024), XY, 0, 0).sum(0)]
    all_gather x0 -> x1, waiting for transfers between devices: none -> 63.8 us  [local(): every = lax.all_gather(projected, 'z').reshape(1024, 512)]
    all_gather x0 -> x1, blocking collectives: none -> 27.1 us  [local(): basis = lax.all_gather(start, 'z').reshape(1024, RX)]
  transfers between devices with their start and end apart: 8 -> 4, of which waited for: 8 -> 3; matrix products, arithmetic and copies ran while one was open for 0% -> 1% of each run, Pallas kernels for 0% -> 0%
where the time goes in v1:
time: 355 us; the launch traced here: 351 us
  blocking collectives  117 us (33%)
  other arithmetic  75.1 us (21%)
  waiting for transfers between devices  72.5 us (20%)
  matrix products  43.1 us (12%)
  starting transfers between devices  15.8 us (4%)
  between operations  14.6 us (4%)
  local copies, waits for them, and re-layouts  13.8 us (4%)
    all_gather x1, waiting for transfers between devices, local(): every = lax.all_gather(projected, 'z').reshape(1024, 512)  63.8 us
    another operation x9, other arithmetic, orthonormal(): lower_factor = jnp.linalg.cholesky(correlation)  37.2 us
    all_to_all x1, blocking collectives, local(): gram = lax.all_to_all(gram.reshape(16, 32, 1024), XY, 0, 0).sum(0)  34 us
    another operation x6, other arithmetic, orthonormal(): lax.linalg.triangular_solve(lower_factor, image_rows, left_side=False, lo...  31.4 us
    all_gather x1, blocking collectives, local(): basis = lax.all_gather(start, 'z').reshape(1024, RX)  27.1 us
    all_to_all x1, blocking collectives, local(): got = lax.all_to_all(send, PLANE, 0, 0).reshape(2, 16, 48, 128)  23.8 us
    all_to_all x1, blocking collectives, local(): gram = lax.all_to_all(gram.reshape(2, 512, 1024), 'c', 0, 0).sum(0)  17.5 us
    dot_general x3, matrix products, local(): basis = orthonormal(jnp.dot(gram, basis, precision=HIGHEST))  14.5 us
  transfers between devices with their start and end apart: 4, of which 3 were waited for; matrix products, arithmetic and copies ran while one was open for 1% of the time, Pallas kernels for 0%

profile of v1, /device:TPU:1, one launch (start us, length us, event | category | flops | bytes accessed | tf_op | source)
XLA Modules:
  0.0 351.4 jit_solution(8924634549707690928)
XLA Ops:
  7.2 0.0 all-gather.2.cloned.1.call-start
  7.2 0.7 convert_element_type.21
  7.9 0.7 convert_element_type.22
  8.6 0.6 multiply_convert_fusion
  9.2 2.3 convert_element_type.24
  11.5 3.7 %convolution_reduce-precision_fusion = f32[128,1024]{1,0:T(8,128)S(1)} fusion(bf16[2048,128]{0,1:T(8,128)(2,1)S(1)} %convert_element_type.24, bf16[1024,2048]{1,0:T(8,128)(2,1)} %bitcast.112), kind=kOutput, calls=%fused_computation.9 | convolution fusion | flops 537001984 | bytes 5242880 | tf_op jit(solution)/shard_map/dot_general | solution.py:45
  15.2 0.1 reshape.77
  15.3 0.1 pad_maximum_fusion
  15.4 23.8 %all_to_all.35 = f32[32,48,128]{2,1,0:T(8,128)S(1)} all-to-all(f32[32,48,128]{2,1,0:T(8,128)S(1)} %pad_maximum_fusion), channel_id=1, replica_groups=mesh['z'=16,'h'=2,'y'=4,'l'=2,'c'=2] {'h','y','l','c'}, dimensions={0} | all-to-all | bytes 1572864 | tf_op jit(solution)/shard_map/all_to_all | solution.py:56
  39.3 0.9 reshape.80
  40.3 2.6 fusion.5
  42.9 0.1 copy.41
  43.0 0.7 all_gather_reshape.6
  43.7 0.0 all-gather.2.cloned.1.call-update
  43.7 63.8 %all-gather.2.cloned.1.call-done = f32[16,64,512]{2,1,0:T(8,128)} async-done(((f32[1,64,512]{2,1,0:T(8,128)}), f32[16,64,512]{2,1,0:T(8,128)}) %all-gather.2.cloned.1.call-update) | async-done | bytes 2097168 | tf_op jit(solution)/shard_map/all_gather | solution.py:64
  107.5 9.5 %fusion.25 = f32[2,512,1024]{2,1,0:T(8,128)S(1)} fusion(f32[2,512,512]{2,1,0:T(8,128)} %bitcast.107, f32[1024,512,1]{1,0,2:T(8,128)} %bitcast.108), kind=kOutput, calls=%fused_computation.43 | convolution fusion | flops 6442450944 | bytes 8388608 | tf_op jit(solution)/shard_map/dot_general | solution.py:65
  117.0 17.5 %all_to_all.36 = f32[2,512,1024]{2,1,0:T(8,128)} all-to-all(f32[2,512,1024]{2,1,0:T(8,128)S(1)} %fusion.25), channel_id=1, replica_groups=mesh['z'=16,'h'=2,'y'=4,'l'=2,'c'=2] {'c'}, dimensions={0} | all-to-all | bytes 8388608 | tf_op jit(solution)/shard_map/all_to_all | solution.py:66
  134.5 2.8 reduce_sum.18
  137.3 34.0 %all_to_all.37 = f32[16,32,1024]{2,1,0:T(8,128)} all-to-all(f32[16,32,1024]{2,1,0:T(8,128)S(1)} %bitcast.110), channel_id=1, replica_groups=mesh['z'=16,'h'=2,'y'=4,'l'=2,'c'=2] {'h','y','l'}, dimensions={0} | all-to-all | bytes 4194304 | tf_op jit(solution)/shard_map/all_to_all | solution.py:67
  171.3 0.6 broadcast_in_dim.14
  171.9 3.5 all-to-all-start.5
  175.4 1.7 reduce_sum.19
  177.1 2.5 all-to-all-done.5
  179.7 1.5 broadcast_in_dim.11
  181.2 4.6 %all-to-all-start.3 = ((f32[16,32,1024]{2,1,0:T(8,128)}), f32[16,32,1024]{2,1,0:T(8,128)}, u32[]{:S(2)}, u32[]{:S(2)}) async-start(f32[16,32,1024]{2,1,0:T(8,128)} %broadcast_in_dim.11), calls=%async_computation.3 | async-start | bytes 4194304 | tf_op jit(solution)/shard_map/all_to_all | solution.py:28
  185.8 27.1 %all_gather.7 = f32[16,64,128]{2,1,0:T(8,128)S(1)} all-gather(f32[1,64,128]{2,1,0:T(8,128)S(1)} %bitcast.118), channel_id=1, replica_groups=mesh['z'=16,'h'=2,'y'=4,'l'=2,'c'=2] {'z'}, dimensions={0}, use_global_device_ids=true | all-gather | bytes 557056 | tf_op jit(solution)/shard_map/all_gather | solution.py:63
  212.9 1.9 copy.45
  214.8 2.3 broadcast_in_dim.13
  217.1 14.1 %all_to_all.38 = f32[2,512,1024]{2,1,0:T(8,128)S(1)} all-to-all(f32[2,512,1024]{2,1,0:T(8,128)S(1)} %broadcast_in_dim.13), channel_id=1, replica_groups=mesh['z'=16,'h'=2,'y'=4,'l'=2,'c'=2] {'c'}, dimensions={0} | all-to-all | bytes 8388608 | tf_op jit(solution)/shard_map/all_to_all | solution.py:28
  231.2 3.4 fusion.26
  234.7 1.0 fusion.27
  235.7 0.1 copy.42
  235.8 11.7 %cholesky.59 = f32[128,128]{1,0:T(8,128)S(1)} custom-call(f32[128,128]{1,0:T(8,128)S(1)} %fusion.19), custom_call_target="Cholesky" | custom-call | tf_op jit(solution)/shard_map/jit(cholesky)/cholesky | solution.py:35
  247.5 0.6 compare_reduce_fusion.2
  248.2 0.7 fusion.11
  248.8 9.8 %custom-call.7 = f32[1,128,128]{1,2,0:T(8,128)S(1)} custom-call(f32[1,128,128]{2,1,0:T(8,128)S(1)} %fusion.11), custom_call_target="InvertDiagBlocksLowerTriangular" | custom-call | tf_op jit(solution)/shard_map/triangular_solve/custom-call.0 | solution.py:36
  258.7 0.6 convolution_bitcast_fusion.2
  259.3 5.7 %fusion.28 = f32[1024,128]{1,0:T(8,128)S(1)} fusion(f32[1024,1024]{1,0:T(8,128)} %bitcast.105, f32[1024,128]{0,1:T(8,128)S(1)} %convolution_bitcast_fusion.2), kind=kOutput, calls=%fused_computation.46 | convolution fusion | flops 1610612736 | bytes 5242880 | tf_op jit(solution)/shard_map/dot_general | solution.py:71
  265.0 1.0 fusion.29
  266.0 0.1 copy.43
  266.1 11.7 %cholesky.70 = f32[128,128]{1,0:T(8,128)S(1)} custom-call(f32[128,128]{1,0:T(8,128)S(1)} %fusion.17), custom_call_target="Cholesky" | custom-call | tf_op jit(solution)/shard_map/jit(cholesky)/cholesky | solution.py:35
  277.9 0.6 compare_reduce_fusion.1
  278.5 0.7 fusion.12
  279.2 9.8 %custom-call.8 = f32[1,128,128]{1,2,0:T(8,128)S(1)} custom-call(f32[1,128,128]{2,1,0:T(8,128)S(1)} %fusion.12), custom_call_target="InvertDiagBlocksLowerTriangular" | custom-call | tf_op jit(solution)/shard_map/triangular_solve/custom-call.0 | solution.py:36
  289.0 0.6 convolution_bitcast_fusion.1
  289.6 5.4 %fusion.30 = f32[1024,128]{1,0:T(8,128)S(1)} fusion(f32[1024,1024]{1,0:T(8,128)} %bitcast.106, f32[1024,128]{0,1:T(8,128)S(1)} %convolution_bitcast_fusion.1), kind=kOutput, calls=%fused_computation.48 | convolution fusion | flops 1610612736 | bytes 5242880 | tf_op jit(solution)/shard_map/dot_general | solution.py:71
  295.0 1.0 fusion.31
  296.1 0.1 copy.44
  296.2 11.7 %cholesky.81 = f32[128,128]{1,0:T(8,128)S(1)} custom-call(f32[128,128]{1,0:T(8,128)S(1)} %fusion.15), custom_call_target="Cholesky" | custom-call | tf_op jit(solution)/shard_map/jit(cholesky)/cholesky | solution.py:35
  307.9 0.6 compare_reduce_fusion
  308.6 0.7 fusion.13
  309.2 9.8 %custom-call.9 = f32[1,128,128]{1,2,0:T(8,128)S(1)} custom-call(f32[1,128,128]{2,1,0:T(8,128)S(1)} %fusion.13), custom_call_target="InvertDiagBlocksLowerTriangular" | custom-call | tf_op jit(solution)/shard_map/triangular_solve/custom-call.0 | solution.py:36
  319.0 0.6 convolution_bitcast_fusion
  319.7 7.8 %fusion.8 = f32[2,16,4,4,8]{1,2,4,3,0:T(4,128)S(1)} fusion(f32[4,16,8,1024]{3,2,1,0:T(8,128)S(1)} %bitcast.111, f32[2,4,1024,1,1]{2,1,0,3,4:T(4,128)S(1)} %reshape.101), kind=kOutput, calls=%fused_computation.11 | convolution fusion | flops 50331648 | bytes 2146304 | tf_op jit(solution)/shard_map/dot_general | solution.py:74
  327.6 0.1 copy.47
  327.7 0.1 reshape.85
  327.8 0.7 copy.48
  328.5 7.7 %all-to-all-start.6 = ((f32[32,1,128]{2,1,0:T(1,128)}), f32[32,1,128]{2,1,0:T(1,128)S(1)}, u32[]{:S(2)}, u32[]{:S(2)}) async-start(f32[32,1,128]{2,1,0:T(1,128)} %copy.48), calls=%async_computation.6 | async-start | bytes 32768 | tf_op jit(solution)/shard_map/all_to_all | solution.py:76
  336.3 0.1 constant_dynamic-slice_fusion
  336.4 0.7 copy.51
  337.1 6.1 %all-to-all-done.6 = f32[32,1,128]{2,1,0:T(1,128)S(1)} async-done(((f32[32,1,128]{2,1,0:T(1,128)}), f32[32,1,128]{2,1,0:T(1,128)S(1)}, u32[]{:S(2)}, u32[]{:S(2)}) %all-to-all-start.6) | async-done | bytes 16416 | tf_op jit(solution)/shard_map/all_to_all | solution.py:76
  343.1 0.1 copy.49
  343.2 0.3 copy.50
  343.5 0.9 reshape.87
  (24 shorter events, 0.3 us)
Async XLA Ops:
  7.2 100.4 %all-gather.2.cloned.1.call-start = ((), (), s32[]{:S(2)}) async-start(), calls=%async_computation.7 | async-start | bytes 2228224 | tf_op jit(solution)/shard_map/all_gather | solution.py:64
  11.5 3.8 %copy-start.4 = (bf16[32,128]{1,0:T(8,128)(2,1)S(1)}, bf16[32,128]{1,0:T(8,128)(2,1)}, u32[]{:S(2)}) copy-start(bf16[32,128]{1,0:T(8,128)(2,1)} %param.9) | copy-start | bytes 24580
  137.3 34.0 %copy-start.3 = (f32[32,128]{1,0:T(8,128)S(1)}, f32[32,128]{1,0:T(8,128)}, u32[]{:S(2)}) copy-start(f32[32,128]{1,0:T(8,128)} %param.12) | copy-start | bytes 49156
  171.9 7.7 %all-to-all-start.5 = ((f32[2,32,128]{2,1,0:T(8,128)}), f32[2,32,128]{2,1,0:T(8,128)S(1)}, u32[]{:S(2)}, u32[]{:S(2)}) async-start(f32[2,32,128]{2,1,0:T(8,128)} %broadcast_in_dim.14), calls=%async_computation.5 | async-start | bytes 65536 | tf_op jit(solution)/shard_map/all_to_all | solution.py:28
  181.2 31.7 %copy-start.1 = (f32[16,64,512]{2,1,0:T(8,128)S(1)}, f32[16,64,512]{2,1,0:T(8,128)}, u32[]{:S(2)}) copy-start(f32[16,64,512]{2,1,0:T(8,128)} %all-gather.2.cloned.1.call-done) | copy-start | bytes 6291460
  181.2 33.5 %all-to-all-start.3 = ((f32[16,32,1024]{2,1,0:T(8,128)}), f32[16,32,1024]{2,1,0:T(8,128)}, u32[]{:S(2)}, u32[]{:S(2)}) async-start(f32[16,32,1024]{2,1,0:T(8,128)} %broadcast_in_dim.11), calls=%async_computation.3 | async-start | bytes 4194304 | tf_op jit(solution)/shard_map/all_to_all | solution.py:28
  231.2 3.4 copy-start
  295.0 24.7 %copy-start.2 = (f32[512,1024]{1,0:T(8,128)S(1)}, f32[512,1024]{1,0:T(8,128)}, u32[]{:S(2)}) copy-start(f32[512,1024]{1,0:T(8,128)} %copy.45) | copy-start | bytes 6291460
  328.5 14.6 %all-to-all-start.6 = ((f32[32,1,128]{2,1,0:T(1,128)}), f32[32,1,128]{2,1,0:T(1,128)S(1)}, u32[]{:S(2)}, u32[]{:S(2)}) async-start(f32[32,1,128]{2,1,0:T(1,128)} %copy.48), calls=%async_computation.6 | async-start | bytes 32768 | tf_op jit(solution)/shard_map/all_to_all | solution.py:76
Sparse Core Ops, SparseCore 0:
  43.8 63.6 all-gather.1

commit v2 on v1

v2 whole, which is shorter than its diff:
```python
import jax
import jax.numpy as jnp
from jax import lax
from jax.experimental import pallas as pl
from jax.experimental.pallas import tpu as pltpu
from jax.sharding import Mesh, PartitionSpec as P

NZ = 64
NV = 32
RX = 128
RY = 128
RZ = 16
RV = 8
ITERS = 3
HIGHEST = lax.Precision.HIGHEST
PLANE = ("h", "y", "l", "c")
XY = ("h", "y", "l")
PART = 168
NN = (((1,), (0,)), ((), ()))
NT = (((1,), (1,)), ((), ()))


def dot(a, b, dims):
    return lax.dot_general(a, b, dims, precision=HIGHEST, preferred_element_type=jnp.float32)


def kronecker_table(z_factor, v_factor):
    table = (
        z_factor.astype(jnp.float32)[:, None, :, None]
        * v_factor.astype(jnp.float32)[None, :, None, :]
    )
    return table.reshape(NZ * NV, RZ * RV).astype(jnp.bfloat16)


def strips_kernel(where_ref, *refs):
    blocks, out_ref = refs[:9], refs[9]
    odd = lax.rem(where_ref[0], 2)
    for t in range(4):
        near = blocks[4 + t][...]
        if t == 0:
            near = near * 0.5
        far = blocks[5 + t][...]
        swap = odd != (t % 2)
        pair = jnp.concatenate([jnp.where(swap, far, near), jnp.where(swap, near, far)], axis=0)
        tile = dot(blocks[4 - t][...], pair, NT)
        for g in range(8):
            out_ref[t * 8 + g, 0:8, :] = tile[8 * g : 8 * g + 8, :]
    last = dot(blocks[0][...], blocks[8][...], NT)
    last = jnp.concatenate([last[:32, :], last[32:, :]], axis=1)
    for p in range(32):
        out_ref[p, 8:16, :] = jnp.broadcast_to(last[p : p + 1, :], (8, 128))


def strips(z, blocks):
    return pl.pallas_call(
        strips_kernel,
        out_shape=jax.ShapeDtypeStruct((32, 16, 128), jnp.float32),
        in_specs=[pl.BlockSpec(memory_space=pltpu.SMEM)]
        + [pl.BlockSpec(memory_space=pltpu.VMEM)] * 9,
        out_specs=pl.BlockSpec(memory_space=pltpu.VMEM),
        compiler_params=pltpu.CompilerParams(vmem_limit_bytes=24 * 1024 * 1024),
        name="strips",
    )(z.reshape(1), *blocks)


def inverse_lower(correlation):
    full = (8, 128)
    sub = lax.broadcasted_iota(jnp.int32, full, 0)
    lane = lax.broadcasted_iota(jnp.int32, full, 1)
    left = [correlation[8 * v : 8 * v + 8, :] for v in range(16)]
    right = [jnp.where(lane == sub + 8 * v, 1.0, 0.0) for v in range(16)]
    done = []

    def row(x, i):
        return jnp.broadcast_to(x[i : i + 1, :], full)

    def column(x, j):
        return jnp.broadcast_to(x[:, j : j + 1], full)

    for v in range(16):
        small = [column(left[v], 8 * v + i) for i in range(8)]
        rest, made = left[v], right[v]
        finished = jnp.zeros(full, jnp.float32)
        for i in range(8):
            pivot = row(small[i], i)
            inverse = 1.0 / pivot
            here = sub == i
            share = jnp.where(here, -inverse, small[i] * inverse)
            made_row = row(made, i)
            root = lax.rsqrt(pivot)
            root = root * (1.5 - 0.5 * pivot * root * root)
            finished = jnp.where(here, made_row * root, finished)
            made = jnp.where(here, 0.0, made) - share * made_row
            if v < 15:
                rest = jnp.where(here, 0.0, rest) - share * row(rest, i)
            for k in range(i + 1, 8):
                small[k] = jnp.where(here, 0.0, small[k]) - share * row(small[k], i)
        done.append(finished)
        if v < 15:
            rest_rows = [row(rest, i) for i in range(8)]
            made_rows = [row(made, i) for i in range(8)]
            for w in range(v + 1, 16):
                shares = [column(left[w], 8 * v + i) for i in range(8)]
                taken = [shares[i] * rest_rows[i] for i in range(8)]
                left[w] = left[w] - (
                    ((taken[0] + taken[1]) + (taken[2] + taken[3]))
                    + ((taken[4] + taken[5]) + (taken[6] + taken[7]))
                )
                taken = [shares[i] * made_rows[i] for i in range(8)]
                right[w] = right[w] - (
                    ((taken[0] + taken[1]) + (taken[2] + taken[3]))
                    + ((taken[4] + taken[5]) + (taken[6] + taken[7]))
                )
    return jnp.concatenate(done, axis=0)


def sweeps_kernel(where_ref, mine, other, every, rows_ref, core_ref, parts, half, far, start, basis, sems):
    z, h, c = where_ref[0], where_ref[1], where_ref[2]
    first = pltpu.make_async_copy(mine, parts.at[c], sems.at[0])
    second = pltpu.make_async_copy(other, parts.at[1 - c], sems.at[1])
    first.start()
    second.start()
    first.wait()
    second.wait()
    lower_lanes = lax.broadcasted_iota(jnp.int32, (8, 128), 1) < 64

    for zz in range(16):
        for hh in range(2):
            for cc in range(2):
                for e in range(2):
                    start[pl.ds(zz * 64 + hh * 32 + 2 * cc + e, 8, stride=4), :] = parts[
                        cc, pl.ds(hh * 8 * PART + 136 + 2 * zz + e, 8, stride=PART), :
                    ]
    for zz in range(16):
        basis[:, zz * 64 : zz * 64 + 64] = start[zz * 64 : zz * 64 + 64, :].T

    for zz in range(8):
        for cc in range(2):
            for g in range(2):
                far[pl.ds(zz * 32 + cc + 16 * g, 8, stride=2), :] = parts[
                    cc, pl.ds(g * 8 * PART + 128 + zz, 8, stride=PART), :
                ]

    def source(row_z, col_z, g):
        d = (col_z - row_z) % 16
        z_of = (row_z + d // 2) % 16
        if d < 8:
            p = (d // 2) * 8 + g
            base = (p // 2) * PART + z_of * 8
            return parts[p % 2, base : base + 8, :]
        if d == 8 and z_of < 8:
            block = far[z_of * 32 + (g % 4) * 8 : z_of * 32 + (g % 4) * 8 + 8, :]
            if (g >= 4) != (col_z % 2 == 1):
                block = pltpu.roll(block, 64, 1)
            return block
        return jnp.zeros((8, 128), jnp.float32)

    for row_z in range(16):
        for pair in range(8):
            for g in range(8):
                a = source(row_z, 2 * pair, g)
                b = source(row_z, 2 * pair + 1, g)
                half[row_z * 64 + g * 8 : row_z * 64 + g * 8 + 8, pair * 128 : pair * 128 + 128] = (
                    jnp.where(lower_lanes, a, b)
                )

    def sweep(_, carry):
        now = basis[...]
        image = dot(now, half[...], NN) + dot(now, half[...], NT)
        correlation = dot(image, image, NT)
        basis[...] = dot(inverse_lower(correlation), image, NN)
        return carry

    lax.fori_loop(0, ITERS, sweep, 0)
    pick = lax.broadcasted_iota(jnp.int32, (32, 1024), 1) == (
        lax.broadcasted_iota(jnp.int32, (32, 1024), 0) + (z * 2 + h) * 32
    )
    rows_ref[...] = dot(jnp.where(pick, 1.0, 0.0), basis[...], NT)
    core_ref[...] = dot(basis[pl.ds(pl.multiple_of(z * 8, 8), 8), :], every[...], NN)


def sweeps(where, mine, other, every):
    return pl.pallas_call(
        sweeps_kernel,
        out_shape=(
            jax.ShapeDtypeStruct((32, RX), jnp.float32),
            jax.ShapeDtypeStruct((8, 512), jnp.float32),
        ),
        in_specs=[
            pl.BlockSpec(memory_space=pltpu.SMEM),
            pl.BlockSpec(memory_space=pl.ANY),
            pl.BlockSpec(memory_space=pl.ANY),
            pl.BlockSpec(memory_space=pltpu.VMEM),
        ],
        out_specs=[pl.BlockSpec(memory_space=pltpu.VMEM)] * 2,
        scratch_shapes=[
            pltpu.VMEM((2, 16 * PART, 128), jnp.float32),
            pltpu.VMEM((1024, 1024), jnp.float32),
            pltpu.VMEM((8 * 32, 128), jnp.float32),
            pltpu.VMEM((1024, 128), jnp.float32),
            pltpu.VMEM((128, 1024), jnp.float32),
            pltpu.SemaphoreType.DMA((2,)),
        ],
        compiler_params=pltpu.CompilerParams(vmem_limit_bytes=48 * 1024 * 1024),
        name="sweeps",
    )(where, mine, other, every)


def local(flow_field, y_factor, z_factor, v_factor, x_start):
    z = lax.axis_index("z").astype(jnp.int32)
    h = lax.axis_index("h").astype(jnp.int32)
    c = lax.axis_index("c").astype(jnp.int32)
    kronecker = kronecker_table(z_factor, v_factor)
    reduced = lax.dot_general(
        kronecker,
        flow_field.reshape(1024, NZ * NV),
        (((0,), (1,)), ((), ())),
        preferred_element_type=jnp.float32,
    )
    reduced = lax.reduce_precision(reduced, 8, 7)
    y_half = lax.dynamic_slice_in_dim(y_factor, h * 16, 16, 0).astype(jnp.float32)
    send = jnp.concatenate(
        [reduced.reshape(32, 32, 128), jnp.broadcast_to(y_half[None], (32, 16, 128))], axis=1
    )
    got = lax.all_to_all(send, PLANE, 0, 0).reshape(2, 16, 48, 128)
    table = got[:, :, 32:, :].transpose(1, 0, 2, 3).reshape(16, 32, 128)
    rows = got[:, :, :32, :].reshape(2, 16, 4, 8, 4, 32)
    projected = jnp.einsum("hgkjay,gyq->hjakq", rows, table, precision=HIGHEST).reshape(64, 512)

    below, above = [projected], [projected]
    from_above = [(i, (i - 1) % 16) for i in range(16)]
    from_below = [(i, (i + 1) % 16) for i in range(16)]
    for _ in range(4):
        above.append(lax.ppermute(above[-1], "z", from_above))
        below.append(lax.ppermute(below[-1], "z", from_below))
    blocks = below[:0:-1] + above
    tied, *_ = lax.optimization_barrier((projected, below[-1], above[-1]))
    every = lax.all_gather(tied, "z").reshape(1024, 512)

    part = lax.all_to_all(strips(z, blocks), PLANE, 0, 0).sum(0)
    gy = (lax.axis_index("y") * 4 + lax.axis_index("l") * 2 + c).astype(jnp.int32)
    start = lax.dynamic_slice_in_dim(x_start, 2 * gy, 2, 0)
    part = jnp.concatenate([part[:9], start, jnp.zeros((5, 128), jnp.float32)], axis=0)
    line = lax.all_gather(part, "z")
    line = jnp.concatenate(
        [line[:, :8].reshape(128, 128), line[:8, 8], line[:, 9:11].reshape(32, 128)], axis=0
    )
    mine = lax.all_to_all(jnp.broadcast_to(line[None], (16, PART, 128)), XY, 0, 0)
    mine = mine.reshape(16 * PART, 128)
    other = lax.ppermute(mine, "c", [(0, 1), (1, 0)])

    x_factor, core = sweeps(jnp.stack([z, h, c]), mine, other, every)
    core = core.reshape(2, 4, 4, 16, 8).transpose(0, 3, 1, 2, 4).reshape(32, 1, 128)
    core = lax.all_to_all(core, PLANE, 0, 0).reshape(32, 4, 4, 8)
    core = core.transpose(1, 3, 0, 2).reshape(4, 1024)
    return (x_factor, core)


def solution(mesh):
    fine = Mesh(mesh.devices.reshape(16, 2, 4, 2, 2), ("z", "h", "y", "l", "c"))
    gx, gy = ("z", "h"), ("y", "l", "c")
    placed = (P(gx, gy, None), P(gy, None), P(), P(), P(gx, None))
    return jax.shard_map(
        local, mesh=fine, in_specs=placed, out_specs=(P(gx, None), P(gx, gy)), check_vma=False
    )
```

time: 355 us -> 217 us (0.61)
  other arithmetic: 75.1 us -> 2.23 us
  waiting for transfers between devices: 72.5 us -> 16.4 us
  Pallas kernels: 0 us -> 42.8 us
  blocking collectives: 117 us -> 75.2 us
  matrix products: 43.1 us -> 6.31 us
  starting transfers between devices: 15.8 us -> 50.8 us
  local copies, waits for them, and re-layouts: 13.8 us -> 7.95 us
    another operation x15 -> x1, other arithmetic: 68.6 us -> 0.08 us  [local(): x_factor, core = sweeps(jnp.stack([z, h, c]), mine, other, every)]
    all_gather x1, waiting for transfers between devices: 63.8 us -> 0.01 us  [local(): every = lax.all_gather(tied, 'z').reshape(1024, 512)]
    pallas_call x0 -> x2, Pallas kernels: none -> 42.8 us  [the longest x1 40.7 us: sweeps(): pl.pallas_call(sweeps_kernel, out_shape=(jax.ShapeDtypeStruct((32, RX), j...]
    ppermute x0 -> x9, starting transfers between devices: none -> 42 us  [the longest x4 25.1 us: local(): above.append(lax.ppermute(above[-1], 'z', from_above))]
    all_to_all x3 -> x2, blocking collectives: 65.7 us -> 30.4 us  [the longest x1 17.9 us: local(): lax.all_to_all(jnp.broadcast_to(line[None], (16, PART, 128)), XY, 0, 0)]
    dot_general x8 -> x0, matrix products: 34.8 us -> none  [the longest x3 14.5 us: local(): basis = orthonormal(jnp.dot(gram, basis, precision=HIGHEST))]
    ppermute x0 -> x9, waiting for transfers between devices: none -> 7.77 us  [the longest x4 5.03 us: local(): below.append(lax.ppermute(below[-1], 'z', from_below))]
    all_to_all x3 -> x1, starting transfers between devices: 15.8 us -> 8.75 us  [local(): part = lax.all_to_all(strips(z, blocks), PLANE, 0, 0).sum(0)]
  transfers between devices with their start and end apart: 4 -> 11, of which waited for: 3 -> 4; matrix products, arithmetic and copies ran while one was open for 1% -> 0% of each run, Pallas kernels for 0% -> 1%
where the time goes in v2:
time: 217 us; the launch traced here: 216 us
  blocking collectives  75.2 us (35%)
  starting transfers between devices  50.8 us (23%)
  Pallas kernels  42.8 us (20%)
  waiting for transfers between devices  16.4 us (8%)
  between operations  14.4 us (7%)
  local copies, waits for them, and re-layouts  7.95 us (4%)
  matrix products  6.31 us (3%)
  other arithmetic  2.23 us (1%)
    pallas_call x1, Pallas kernels, sweeps(): pl.pallas_call(sweeps_kernel, out_shape=(jax.ShapeDtypeStruct((32, RX), j...  40.7 us
    ppermute x4, starting transfers between devices, local(): above.append(lax.ppermute(above[-1], 'z', from_above))  25.1 us
    all_to_all x1, blocking collectives, local(): got = lax.all_to_all(send, PLANE, 0, 0).reshape(2, 16, 48, 128)  23.6 us
    all_gather x1, blocking collectives, local(): line = lax.all_gather(part, 'z')  21.1 us
    all_to_all x1, blocking collectives, local(): lax.all_to_all(jnp.broadcast_to(line[None], (16, PART, 128)), XY, 0, 0)  17.9 us
    all_to_all x1, blocking collectives, local(): core = lax.all_to_all(core, PLANE, 0, 0).reshape(32, 4, 4, 8)  12.5 us
    ppermute x1, starting transfers between devices, local(): other = lax.ppermute(mine, 'c', [(0, 1), (1, 0)])  9.22 us
    all_to_all x1, starting transfers between devices, local(): part = lax.all_to_all(strips(z, blocks), PLANE, 0, 0).sum(0)  8.75 us
  transfers between devices with their start and end apart: 11, of which 4 were waited for; matrix products, arithmetic and copies ran while one was open for 0% of the time, Pallas kernels for 1%

profile of v2, /device:TPU:1, one launch (start us, length us, event | category | flops | bytes accessed | tf_op | source)
XLA Modules:
  0.0 216.0 jit_solution(16645181983811445029)
XLA Ops:
  7.2 0.0 copy-start
  7.2 0.0 all-gather.4.cloned.1.call-start
  7.2 0.7 convert_element_type.22
  7.9 0.7 convert_element_type.21
  8.6 0.6 multiply_convert_fusion
  9.2 2.3 %convert_element_type.24 = bf16[2048,128]{0,1:T(8,128)(2,1)S(1)} reshape(bf16[64,32,16,8]{1,0,3,2:T(8,128)(2,1)S(1)} %multiply_convert_fusion) | data formatting | bytes 1048576 | tf_op jit(solution)/shard_map/convert_element_type | solution.py:32
  11.5 0.0 copy-start.4
  11.5 3.7 %convolution_reduce-precision_fusion = f32[128,1024]{1,0:T(8,128)S(1)} fusion(bf16[2048,128]{0,1:T(8,128)(2,1)S(1)} %convert_element_type.24, bf16[1024,2048]{1,0:T(8,128)(2,1)} %bitcast.52), kind=kOutput, calls=%fused_computation.3 | convolution fusion | flops 537001984 | bytes 5242880 | tf_op jit(solution)/shard_map/dot_general | solution.py:214
  15.2 0.1 reshape.65
  15.3 0.0 copy-done.4
  15.3 0.1 pad_maximum_fusion
  15.4 23.6 %all_to_all.20 = f32[32,48,128]{2,1,0:T(8,128)S(1)} all-to-all(f32[32,48,128]{2,1,0:T(8,128)S(1)} %pad_maximum_fusion), channel_id=1, replica_groups=mesh['z'=16,'h'=2,'y'=4,'l'=2,'c'=2] {'h','y','l','c'}, dimensions={0} | all-to-all | bytes 1572864 | tf_op jit(solution)/shard_map/all_to_all | solution.py:225
  39.1 0.1 slice.25
  39.2 0.9 reshape.68
  40.1 2.6 %fusion.2 = f32[2,8,4,4,128]{4,1,2,3,0:T(8,128)S(1)} fusion(f32[16,32,128,1,1,1]{2,1,0,5,4,3:T(8,128)S(1)} %bitcast.55, f32[2,16,4,8,4,32]{5,4,3,2,1,0:T(4,128)S(1)} %reshape.68), kind=kOutput, calls=%fused_computation.4 | convolution fusion | flops 201326592 | bytes 917504 | tf_op jit(solution)/shard_map/hgkjay,gyq->hjakq/dot_general | solution.py:228
  42.7 0.1 copy.19
  42.8 0.0 copy-start.2
  42.8 9.9 %collective-permute-start.4 = (f32[64,512]{1,0:T(8,128)S(1)}, f32[64,512]{1,0:T(8,128)S(1)}, u32[]{:S(2)}, u32[]{:S(2)}) collective-permute-start(f32[64,512]{1,0:T(8,128)S(1)} %bitcast.48), channel_id=1, source_target_pairs={{0,480},{32,0},{64,32},{96,64},{128,96},{160,128},{192,160},{224,1... | collective-permute-start | bytes 393224 | tf_op jit(solution)/shard_map/ppermute | solution.py:234
  52.7 1.9 collective-permute-start
  54.6 0.3 collective-permute-done.4.refs_5_
  54.9 5.3 %collective-permute-start.5 = (f32[64,512]{1,0:T(8,128)S(1)}, f32[64,512]{1,0:T(8,128)S(1)}, u32[]{:S(2)}, u32[]{:S(2)}) collective-permute-start(f32[64,512]{1,0:T(8,128)S(1)} %collective-permute-done.4.refs_5_), channel_id=1, source_target_pairs={{0,480},{32,0},{64,32},{96,64},{128,96},{160,128},{192,160},{224,1... | collective-permute-start | bytes 393224 | tf_op jit(solution)/shard_map/ppermute | solution.py:234
  60.2 0.0 collective-permute-done.refs_3_
  60.2 1.9 collective-permute-start.1
  62.1 0.0 collective-permute-done.5.refs_6_
  62.1 5.0 %collective-permute-start.6 = (f32[64,512]{1,0:T(8,128)S(1)}, f32[64,512]{1,0:T(8,128)S(1)}, u32[]{:S(2)}, u32[]{:S(2)}) collective-permute-start(f32[64,512]{1,0:T(8,128)S(1)} %collective-permute-done.5.refs_6_), channel_id=1, source_target_pairs={{0,480},{32,0},{64,32},{96,64},{128,96},{160,128},{192,160},{224,1... | collective-permute-start | bytes 393224 | tf_op jit(solution)/shard_map/ppermute | solution.py:234
  67.1 0.0 collective-permute-done.1.refs_2_
  67.1 1.9 collective-permute-start.2
  69.1 0.0 collective-permute-done.6.refs_7_
  69.1 5.0 %collective-permute-start.7 = (f32[64,512]{1,0:T(8,128)S(1)}, f32[64,512]{1,0:T(8,128)S(1)}, u32[]{:S(2)}, u32[]{:S(2)}) collective-permute-start(f32[64,512]{1,0:T(8,128)S(1)} %collective-permute-done.6.refs_7_), channel_id=1, source_target_pairs={{0,480},{32,0},{64,32},{96,64},{128,96},{160,128},{192,160},{224,1... | collective-permute-start | bytes 393224 | tf_op jit(solution)/shard_map/ppermute | solution.py:234
  74.0 0.0 collective-permute-done.2.refs_1_
  74.0 1.9 collective-permute-start.3
  76.0 0.0 collective-permute-done.7.refs_8_
  76.0 5.0 %collective-permute-done.3.refs_0_ = f32[64,512]{1,0:T(8,128)S(1)} collective-permute-done((f32[64,512]{1,0:T(8,128)S(1)}, f32[64,512]{1,0:T(8,128)S(1)}, u32[]{:S(2)}, u32[]{:S(2)}) %collective-permute-start.3) | collective-permute-done | bytes 131104 | tf_op jit(solution)/shard_map/ppermute | solution.py:235
  81.0 0.0 copy-done.2
  81.0 0.0 all-gather.4.cloned.1.call-update
  81.0 0.0 copy-start.3
  81.0 0.9 copy-done.3
  81.9 2.1 strips.1
  84.0 8.7 %all-to-all-start.1 = ((f32[32,16,128]{2,1,0:T(8,128)}), f32[32,16,128]{2,1,0:T(8,128)S(1)}, u32[]{:S(2)}, u32[]{:S(2)}) async-start(f32[32,16,128]{2,1,0:T(8,128)} %strips.1), calls=%async_computation.1 | async-start | bytes 524288 | tf_op jit(solution)/shard_map/all_to_all | solution.py:240
  92.8 0.1 pad.5.clone
  92.9 0.0 copy-done
  92.9 8.6 %all-to-all-done.1 = f32[32,16,128]{2,1,0:T(8,128)S(1)} async-done(((f32[32,16,128]{2,1,0:T(8,128)}), f32[32,16,128]{2,1,0:T(8,128)S(1)}, u32[]{:S(2)}, u32[]{:S(2)}) %all-to-all-start.1) | async-done | bytes 262176 | tf_op jit(solution)/shard_map/all_to_all | solution.py:240
  101.5 0.1 maximum_maximum_fusion
  101.5 21.1 %all-gather = f32[256,128]{1,0:T(8,128)S(1)} all-gather(f32[16,128]{1,0:T(8,128)S(1)} %maximum_maximum_fusion), channel_id=2, replica_groups=mesh['z'=16,'h'=2,'y'=4,'l'=2,'c'=2] {'z'}, dimensions={0}, use_global_device_ids=true | all-gather | bytes 139264 | tf_op jit(solution)/shard_map/all_gather | solution.py:244
  122.7 0.1 broadcast_in_dim.8
  122.8 17.9 %all_to_all.21 = f32[16,168,128]{2,1,0:T(8,128)S(1)} all-to-all(f32[16,168,128]{2,1,0:T(8,128)S(1)} %broadcast_in_dim.8), channel_id=1, replica_groups=mesh['z'=16,'h'=2,'y'=4,'l'=2,'c'=2] {'h','y','l'}, dimensions={0} | all-to-all | bytes 2752512 | tf_op jit(solution)/shard_map/all_to_all | solution.py:248
  140.7 9.2 %collective-permute-start.8 = (f32[2688,128]{1,0:T(8,128)S(1)}, f32[2688,128]{1,0:T(8,128)S(1)}, u32[]{:S(2)}, u32[]{:S(2)}) collective-permute-start(f32[2688,128]{1,0:T(8,128)S(1)} %bitcast.46), channel_id=1, source_target_pairs={{0,1},{1,0},{2,3},{3,2},{4,5},{5,4},{6,7},{7,6},{8,9},{9,8},{10,11... | collective-permute-start | bytes 4128776 | tf_op jit(solution)/shard_map/ppermute | solution.py:250
  149.9 0.1 pad_add_fusion.where_ref
  150.0 2.5 %collective-permute-done.8.other = f32[2688,128]{1,0:T(8,128)S(1)} collective-permute-done((f32[2688,128]{1,0:T(8,128)S(1)}, f32[2688,128]{1,0:T(8,128)S(1)}, u32[]{:S(2)}, u32[]{:S(2)}) %collective-permute-start.8) | collective-permute-done | bytes 1376288 | tf_op jit(solution)/shard_map/ppermute | solution.py:250
  152.5 0.0 all-gather.4.cloned.1.call-done.every
  152.5 0.0 copy-start.1
  152.5 1.6 copy-done.1
  154.1 40.7 %sweeps.1 = (f32[32,128]{1,0:T(8,128)}, f32[8,512]{1,0:T(8,128)S(1)}) custom-call(s32[3]{0:T(128)S(1)} %pad_add_fusion.where_ref, f32[2688,128]{1,0:T(8,128)S(1)} %bitcast.47, f32[2688,128]{1,0:T(8,128)S(1)} %collective-permute-done.8.other, f32[1024,512]{1,0:T(8,128)S(1)} %copy-done.1), custom_call_target="tpu_custom_call" | custom-call | tf_op jit(solution)/shard_map/sweeps/pallas_call | solution.py:183
  194.8 0.2 reshape.74
  195.0 0.2 copy.20
  195.1 0.1 reshape.75
  195.3 0.1 copy.21
  195.3 12.5 %all_to_all.22 = f32[32,1,128]{2,1,0:T(1,128)S(1)} all-to-all(f32[32,1,128]{2,1,0:T(1,128)S(1)} %copy.21), channel_id=1, replica_groups=mesh['z'=16,'h'=2,'y'=4,'l'=2,'c'=2] {'h','y','l','c'}, dimensions={0} | all-to-all | bytes 32768 | tf_op jit(solution)/shard_map/all_to_all | solution.py:254
  207.9 0.1 copy.22
  207.9 0.3 copy.23
  208.2 0.9 reshape.77
  (12 shorter events, 0.2 us)
Async XLA Ops:
  7.2 85.7 %copy-start = (f32[32,128]{1,0:T(8,128)S(1)}, f32[32,128]{1,0:T(8,128)}, u32[]{:S(2)}) copy-start(f32[32,128]{1,0:T(8,128)} %param.9) | copy-start | bytes 49156
  7.2 145.3 %all-gather.4.cloned.1.call-start = ((), (), s32[]{:S(2)}) async-start(), calls=%async_computation.4 | async-start | bytes 2228224 | tf_op jit(solution)/shard_map/all_gather | solution.py:238
  11.5 3.8 %copy-start.4 = (bf16[32,128]{1,0:T(8,128)(2,1)S(1)}, bf16[32,128]{1,0:T(8,128)(2,1)}, u32[]{:S(2)}) copy-start(bf16[32,128]{1,0:T(8,128)(2,1)} %param.6) | copy-start | bytes 24580
  42.8 38.2 %copy-start.2 = (f32[8,8,4,128]{3,1,2,0:T(8,128)}, f32[8,8,4,128]{3,1,2,0:T(8,128)S(1)}, u32[]{:S(2)}) copy-start(f32[8,8,4,128]{3,1,2,0:T(8,128)S(1)} %copy.32) | copy-start | bytes 393220
  42.8 12.1 %collective-permute-start.4 = (f32[64,512]{1,0:T(8,128)S(1)}, f32[64,512]{1,0:T(8,128)S(1)}, u32[]{:S(2)}, u32[]{:S(2)}) collective-permute-start(f32[64,512]{1,0:T(8,128)S(1)} %bitcast.48), channel_id=1, source_target_pairs={{0,480},{32,0},{64,32},{96,64},{128,96},{160,128},{192,160},{224,1... | collective-permute-start | bytes 393224 | tf_op jit(solution)/shard_map/ppermute | solution.py:234
  52.7 7.5 %collective-permute-start = (f32[64,512]{1,0:T(8,128)S(1)}, f32[64,512]{1,0:T(8,128)S(1)}, u32[]{:S(2)}, u32[]{:S(2)}) collective-permute-start(f32[64,512]{1,0:T(8,128)S(1)} %bitcast.49), channel_id=1, source_target_pairs={{0,32},{32,64},{64,96},{96,128},{128,160},{160,192},{192,224},{224... | collective-permute-start | bytes 393224 | tf_op jit(solution)/shard_map/ppermute | solution.py:235
  54.9 7.3 %collective-permute-start.5 = (f32[64,512]{1,0:T(8,128)S(1)}, f32[64,512]{1,0:T(8,128)S(1)}, u32[]{:S(2)}, u32[]{:S(2)}) collective-permute-start(f32[64,512]{1,0:T(8,128)S(1)} %collective-permute-done.4.refs_5_), channel_id=1, source_target_pairs={{0,480},{32,0},{64,32},{96,64},{128,96},{160,128},{192,160},{224,1... | collective-permute-start | bytes 393224 | tf_op jit(solution)/shard_map/ppermute | solution.py:234
  60.2 6.9 %collective-permute-start.1 = (f32[64,512]{1,0:T(8,128)S(1)}, f32[64,512]{1,0:T(8,128)S(1)}, u32[]{:S(2)}, u32[]{:S(2)}) collective-permute-start(f32[64,512]{1,0:T(8,128)S(1)} %collective-permute-done.refs_3_), channel_id=1, source_target_pairs={{0,32},{32,64},{64,96},{96,128},{128,160},{160,192},{192,224},{224... | collective-permute-start | bytes 393224 | tf_op jit(solution)/shard_map/ppermute | solution.py:235
  62.1 6.9 %collective-permute-start.6 = (f32[64,512]{1,0:T(8,128)S(1)}, f32[64,512]{1,0:T(8,128)S(1)}, u32[]{:S(2)}, u32[]{:S(2)}) collective-permute-start(f32[64,512]{1,0:T(8,128)S(1)} %collective-permute-done.5.refs_6_), channel_id=1, source_target_pairs={{0,480},{32,0},{64,32},{96,64},{128,96},{160,128},{192,160},{224,1... | collective-permute-start | bytes 393224 | tf_op jit(solution)/shard_map/ppermute | solution.py:234
  67.1 6.9 %collective-permute-start.2 = (f32[64,512]{1,0:T(8,128)S(1)}, f32[64,512]{1,0:T(8,128)S(1)}, u32[]{:S(2)}, u32[]{:S(2)}) collective-permute-start(f32[64,512]{1,0:T(8,128)S(1)} %collective-permute-done.1.refs_2_), channel_id=1, source_target_pairs={{0,32},{32,64},{64,96},{96,128},{128,160},{160,192},{192,224},{224... | collective-permute-start | bytes 393224 | tf_op jit(solution)/shard_map/ppermute | solution.py:235
  69.1 6.9 %collective-permute-start.7 = (f32[64,512]{1,0:T(8,128)S(1)}, f32[64,512]{1,0:T(8,128)S(1)}, u32[]{:S(2)}, u32[]{:S(2)}) collective-permute-start(f32[64,512]{1,0:T(8,128)S(1)} %collective-permute-done.6.refs_7_), channel_id=1, source_target_pairs={{0,480},{32,0},{64,32},{96,64},{128,96},{160,128},{192,160},{224,1... | collective-permute-start | bytes 393224 | tf_op jit(solution)/shard_map/ppermute | solution.py:234
  74.0 6.9 %collective-permute-start.3 = (f32[64,512]{1,0:T(8,128)S(1)}, f32[64,512]{1,0:T(8,128)S(1)}, u32[]{:S(2)}, u32[]{:S(2)}) collective-permute-start(f32[64,512]{1,0:T(8,128)S(1)} %collective-permute-done.2.refs_1_), channel_id=1, source_target_pairs={{0,32},{32,64},{64,96},{96,128},{128,160},{160,192},{192,224},{224... | collective-permute-start | bytes 393224 | tf_op jit(solution)/shard_map/ppermute | solution.py:235
  81.0 0.9 copy-start.3
  84.0 17.4 %all-to-all-start.1 = ((f32[32,16,128]{2,1,0:T(8,128)}), f32[32,16,128]{2,1,0:T(8,128)S(1)}, u32[]{:S(2)}, u32[]{:S(2)}) async-start(f32[32,16,128]{2,1,0:T(8,128)} %strips.1), calls=%async_computation.1 | async-start | bytes 524288 | tf_op jit(solution)/shard_map/all_to_all | solution.py:240
  140.7 11.8 %collective-permute-start.8 = (f32[2688,128]{1,0:T(8,128)S(1)}, f32[2688,128]{1,0:T(8,128)S(1)}, u32[]{:S(2)}, u32[]{:S(2)}) collective-permute-start(f32[2688,128]{1,0:T(8,128)S(1)} %bitcast.46), channel_id=1, source_target_pairs={{0,1},{1,0},{2,3},{3,2},{4,5},{5,4},{6,7},{7,6},{8,9},{9,8},{10,11... | collective-permute-start | bytes 4128776 | tf_op jit(solution)/shard_map/ppermute | solution.py:250
  152.5 1.6 copy-start.1
Sparse Core Ops, SparseCore 0:
  81.1 61.0 all-gather.3

commit v3 on v2

--- a/solution.py
+++ b/solution.py
@@ -18,18 +18,94 @@
 PART = 168
 NN = (((1,), (0,)), ((), ()))
 NT = (((1,), (1,)), ((), ()))
+TN = (((0,), (0,)), ((), ()))
+BLOCKS = 4
 
 
 def dot(a, b, dims):
     return lax.dot_general(a, b, dims, precision=HIGHEST, preferred_element_type=jnp.float32)
 
 
-def kronecker_table(z_factor, v_factor):
-    table = (
-        z_factor.astype(jnp.float32)[:, None, :, None]
-        * v_factor.astype(jnp.float32)[None, :, None, :]
-    )
-    return table.reshape(NZ * NV, RZ * RV).astype(jnp.bfloat16)
+def reduced_kernel(where_ref, flow, y_ref, z_ref, v_ref, out_ref, held, table, turned, sems):
+    size = 1024 // BLOCKS
+
+    def fetch(j):
+        return pltpu.make_async_copy(flow.at[pl.ds(size * j, size), :], held.at[j], sems.at[j])
+
+    for j in range(BLOCKS):
+        fetch(j).start()
+    wide = lax.broadcasted_iota(jnp.int32, (RZ, 128), 1) // RV == lax.broadcasted_iota(jnp.int32, (RZ, 128), 0)
+    z_wide = lax.dot_general(z_ref[...], wide.astype(jnp.bfloat16), TN, preferred_element_type=jnp.float32)
+    wide = lax.broadcasted_iota(jnp.int32, (RV, 128), 1) % RV == lax.broadcasted_iota(jnp.int32, (RV, 128), 0)
+    v_wide = lax.dot_general(v_ref[...], wide.astype(jnp.bfloat16), TN, preferred_element_type=jnp.float32)
+    for i in range(NZ):
+        table[NV * i : NV * i + NV, :] = (z_wide[i : i + 1, :] * v_wide).astype(jnp.bfloat16)
+    half = y_ref[pl.ds(pl.multiple_of(where_ref[0] * 16, 16), 16), :].astype(jnp.float32)
+    for p in range(32):
+        out_ref[p * 48 + 32 : p * 48 + 48, :] = half
+    for i in range(BLOCKS):
+        fetch(i).wait()
+        block = lax.dot_general(held[i], table[...], NN, preferred_element_type=jnp.float32)
+        for part in range(size // 128):
+            j = i * (size // 128) + part
+            turned[...] = block[part * 128 : part * 128 + 128, :].T.astype(jnp.bfloat16).astype(jnp.float32)
+            for k in range(4):
+                out_ref[pl.ds(k * 8 + j, 32, stride=48), :] = turned[pl.ds(k, 32, stride=4), :]
+
+
+def reduced_blocks(where, flow, y_factor, z_factor, v_factor):
+    return pl.pallas_call(
+        reduced_kernel,
+        out_shape=jax.ShapeDtypeStruct((32 * 48, 128), jnp.float32),
+        in_specs=[pl.BlockSpec(memory_space=pltpu.SMEM), pl.BlockSpec(memory_space=pl.ANY)]
+        + [pl.BlockSpec(memory_space=pltpu.VMEM)] * 3,
+        out_specs=pl.BlockSpec(memory_space=pltpu.VMEM),
+        scratch_shapes=[
+            pltpu.VMEM((BLOCKS, 1024 // BLOCKS, NZ * NV), jnp.bfloat16),
+            pltpu.VMEM((NZ * NV, 128), jnp.bfloat16),
+            pltpu.VMEM((128, 128), jnp.float32),
+            pltpu.SemaphoreType.DMA((BLOCKS,)),
+        ],
+        compiler_params=pltpu.CompilerParams(vmem_limit_bytes=56 * 1024 * 1024),
+        name="reduced_blocks",
+    )(where, flow, y_factor, z_factor, v_factor)
+
+
+def projected_kernel(got, out_ref, ordered):
+    quarter = lax.broadcasted_iota(jnp.int32, (64, 128), 1) // 32
+    total = jnp.zeros((256, 128), jnp.float32)
+    for gy in range(0, 16, 2):
+        rows, table = [], []
+        for g in (gy, gy + 1):
+            low, high = g * 48, (16 + g) * 48
+            block = jnp.concatenate([got[low : low + 32, :], got[high : high + 32, :]], axis=0)
+            rows.append(
+                jnp.concatenate([jnp.where(quarter == a, block, 0.0) for a in range(4)], axis=0)
+            )
+            factor = jnp.concatenate([got[low + 32 : low + 48, :], got[high + 32 : high + 48, :]], axis=0)
+            table += [factor] * 4
+        rows = jnp.concatenate(rows, axis=1).astype(jnp.bfloat16)
+        table = jnp.concatenate(table, axis=0).astype(jnp.bfloat16)
+        total = total + lax.dot_general(rows, table, NN, preferred_element_type=jnp.float32)
+    for a in range(4):
+        for h in range(2):
+            for k in range(4):
+                base = a * 64 + h * 32 + k * 8
+                ordered[pl.ds(k * 64 + h * 32 + a, 8, stride=4), :] = total[base : base + 8, :]
+    for k in range(4):
+        out_ref[:, k * 128 : k * 128 + 128] = ordered[k * 64 : k * 64 + 64, :]
+
+
+def projected_rows(got):
+    return pl.pallas_call(
+        projected_kernel,
+        out_shape=jax.ShapeDtypeStruct((64, 512), jnp.float32),
+        in_specs=[pl.BlockSpec(memory_space=pltpu.VMEM)],
+        out_specs=pl.BlockSpec(memory_space=pltpu.VMEM),
+        scratch_shapes=[pltpu.VMEM((256, 128), jnp.float32)],
+        compiler_params=pltpu.CompilerParams(vmem_limit_bytes=16 * 1024 * 1024),
+        name="projected_rows",
+    )(got)
 
 
 def strips_kernel(where_ref, *refs):
@@ -67,9 +143,6 @@
     full = (8, 128)
     sub = lax.broadcasted_iota(jnp.int32, full, 0)
     lane = lax.broadcasted_iota(jnp.int32, full, 1)
-    left = [correlation[8 * v : 8 * v + 8, :] for v in range(16)]
-    right = [jnp.where(lane == sub + 8 * v, 1.0, 0.0) for v in range(16)]
-    done = []
 
     def row(x, i):
         return jnp.broadcast_to(x[i : i + 1, :], full)
@@ -77,44 +150,60 @@
     def column(x, j):
         return jnp.broadcast_to(x[:, j : j + 1], full)
 
+    def total(t):
+        return ((t[0] + t[1]) + (t[2] + t[3])) + ((t[4] + t[5]) + (t[6] + t[7]))
+
+    left = [correlation[8 * v : 8 * v + 8, :] for v in range(16)]
+    eye = [lane == sub + 8 * v for v in range(16)]
+    on = [jnp.where(eye[v], left[v], 0.0) for v in range(16)]
+    acc = on[0]
+    for v in range(1, 16):
+        acc = acc + on[v]
+    across = lax.rsqrt(jnp.broadcast_to(jnp.sum(acc, axis=0, keepdims=True), full))
+    down = [lax.rsqrt(jnp.broadcast_to(jnp.sum(on[v], axis=1, keepdims=True), full)) for v in range(16)]
+    left = [left[v] * across * down[v] for v in range(16)]
+    right = [jnp.where(eye[v], across, 0.0) for v in range(16)]
+    done = []
     for v in range(16):
         small = [column(left[v], 8 * v + i) for i in range(8)]
         rest, made = left[v], right[v]
         finished = jnp.zeros(full, jnp.float32)
-        for i in range(8):
-            pivot = row(small[i], i)
-            inverse = 1.0 / pivot
-            here = sub == i
-            share = jnp.where(here, -inverse, small[i] * inverse)
-            made_row = row(made, i)
-            root = lax.rsqrt(pivot)
-            root = root * (1.5 - 0.5 * pivot * root * root)
-            finished = jnp.where(here, made_row * root, finished)
-            made = jnp.where(here, 0.0, made) - share * made_row
+        for i in (0, 2, 4, 6):
+            j = i + 1
+            a, b, d = row(small[i], i), row(small[i], j), row(small[j], j)
+            inverse = 1.0 / (a * d - b * b)
+            ia, ib, id_ = d * inverse, b * inverse, a * inverse
+            at_i, at_j = sub == i, sub == j
+            here = jnp.logical_or(at_i, at_j)
+            share_i = jnp.where(at_i, -ia, jnp.where(at_j, ib, small[i] * ia - small[j] * ib))
+            share_j = jnp.where(at_i, ib, jnp.where(at_j, -id_, small[j] * id_ - small[i] * ib))
+            made_i, made_j = row(made, i), row(made, j)
+            root = lax.rsqrt(a)
+            root = root * (1.5 - 0.5 * a * root * root)
+            ratio = b * root * root
+            left_over = d - b * ratio
+            second = lax.rsqrt(left_over)
+            second = second * (1.5 - 0.5 * left_over * second * second)
+            finished = jnp.where(at_i, made_i * root, jnp.where(at_j, (made_j - ratio * made_i) * second, finished))
+            def less(x, x_i, x_j):
+                return jnp.where(here, 0.0, x) - (share_i * x_i + share_j * x_j)
+            made = less(made, made_i, made_j)
             if v < 15:
-                rest = jnp.where(here, 0.0, rest) - share * row(rest, i)
-            for k in range(i + 1, 8):
-                small[k] = jnp.where(here, 0.0, small[k]) - share * row(small[k], i)
+                rest = less(rest, row(rest, i), row(rest, j))
+            for k in range(i + 2, 8):
+                small[k] = less(small[k], row(small[k], i), row(small[k], j))
         done.append(finished)
         if v < 15:
             rest_rows = [row(rest, i) for i in range(8)]
             made_rows = [row(made, i) for i in range(8)]
             for w in range(v + 1, 16):
                 shares = [column(left[w], 8 * v + i) for i in range(8)]
-                taken = [shares[i] * rest_rows[i] for i in range(8)]
-                left[w] = left[w] - (
-                    ((taken[0] + taken[1]) + (taken[2] + taken[3]))
-                    + ((taken[4] + taken[5]) + (taken[6] + taken[7]))
-                )
-                taken = [shares[i] * made_rows[i] for i in range(8)]
-                right[w] = right[w] - (
-                    ((taken[0] + taken[1]) + (taken[2] + taken[3]))
-                    + ((taken[4] + taken[5]) + (taken[6] + taken[7]))
-                )
+                left[w] = left[w] - total([shares[i] * rest_rows[i] for i in range(8)])
+                right[w] = right[w] - total([shares[i] * made_rows[i] for i in range(8)])
     return jnp.concatenate(done, axis=0)
 
 
-def sweeps_kernel(where_ref, mine, other, every, rows_ref, core_ref, parts, half, far, start, basis, sems):
+def sweeps_kernel(where_ref, mine, other, rows_ref, cols_ref, parts, half, far, start, basis, sems):
     z, h, c = where_ref[0], where_ref[1], where_ref[2]
     first = pltpu.make_async_copy(mine, parts.at[c], sems.at[0])
     second = pltpu.make_async_copy(other, parts.at[1 - c], sems.at[1])
@@ -163,10 +252,16 @@
                 half[row_z * 64 + g * 8 : row_z * 64 + g * 8 + 8, pair * 128 : pair * 128 + 128] = (
                     jnp.where(lower_lanes, a, b)
                 )
+    for i in range(8):
+        for j in range(i + 1):
+            rows, cols = slice(i * 128, i * 128 + 128), slice(j * 128, j * 128 + 128)
+            block = half[rows, cols] + half[cols, rows].T
+            half[rows, cols] = block
+            if i != j:
+                half[cols, rows] = block.T
 
     def sweep(_, carry):
-        now = basis[...]
-        image = dot(now, half[...], NN) + dot(now, half[...], NT)
+        image = dot(basis[...], half[...], NN)
         correlation = dot(image, image, NT)
         basis[...] = dot(inverse_lower(correlation), image, NN)
         return carry
@@ -176,21 +271,35 @@
         lax.broadcasted_iota(jnp.int32, (32, 1024), 0) + (z * 2 + h) * 32
     )
     rows_ref[...] = dot(jnp.where(pick, 1.0, 0.0), basis[...], NT)
-    core_ref[...] = dot(basis[pl.ds(pl.multiple_of(z * 8, 8), 8), :], every[...], NN)
-
-
-def sweeps(where, mine, other, every):
+    cols_ref[...] = basis[pl.ds(pl.multiple_of(z * 8, 8), 8), :]
+
+
+def core_kernel(cols_ref, every_ref, core_ref):
+    core_ref[...] = dot(cols_ref[...], every_ref[...], NN)
+
+
+def core_rows(cols, every):
+    return pl.pallas_call(
+        core_kernel,
+        out_shape=jax.ShapeDtypeStruct((8, 512), jnp.float32),
+        in_specs=[pl.BlockSpec(memory_space=pltpu.VMEM)] * 2,
+        out_specs=pl.BlockSpec(memory_space=pltpu.VMEM),
+        compiler_params=pltpu.CompilerParams(vmem_limit_bytes=16 * 1024 * 1024),
+        name="core_rows",
+    )(cols, every)
+
+
+def sweeps(where, mine, other):
     return pl.pallas_call(
         sweeps_kernel,
         out_shape=(
             jax.ShapeDtypeStruct((32, RX), jnp.float32),
-            jax.ShapeDtypeStruct((8, 512), jnp.float32),
+            jax.ShapeDtypeStruct((8, 1024), jnp.float32),
         ),
         in_specs=[
             pl.BlockSpec(memory_space=pltpu.SMEM),
             pl.BlockSpec(memory_space=pl.ANY),
             pl.BlockSpec(memory_space=pl.ANY),
-            pl.BlockSpec(memory_space=pltpu.VMEM),
         ],
         out_specs=[pl.BlockSpec(memory_space=pltpu.VMEM)] * 2,
         scratch_shapes=[
@@ -201,40 +310,31 @@
             pltpu.VMEM((128, 1024), jnp.float32),
             pltpu.SemaphoreType.DMA((2,)),
         ],
-        compiler_params=pltpu.CompilerParams(vmem_limit_bytes=48 * 1024 * 1024),
+        compiler_params=pltpu.CompilerParams(vmem_limit_bytes=32 * 1024 * 1024),
         name="sweeps",
-    )(where, mine, other, every)
+    )(where, mine, other)
 
 
 def local(flow_field, y_factor, z_factor, v_factor, x_start):
     z = lax.axis_index("z").astype(jnp.int32)
     h = lax.axis_index("h").astype(jnp.int32)
     c = lax.axis_index("c").astype(jnp.int32)
-    kronecker = kronecker_table(z_factor, v_factor)
-    reduced = lax.dot_general(
-        kronecker,
-        flow_field.reshape(1024, NZ * NV),
-        (((0,), (1,)), ((), ())),
-        preferred_element_type=jnp.float32,
+    send = reduced_blocks(
+        h.reshape(1), flow_field.reshape(1024, NZ * NV), y_factor, z_factor.T, v_factor.T
     )
-    reduced = lax.reduce_precision(reduced, 8, 7)
-    y_half = lax.dynamic_slice_in_dim(y_factor, h * 16, 16, 0).astype(jnp.float32)
-    send = jnp.concatenate(
-        [reduced.reshape(32, 32, 128), jnp.broadcast_to(y_half[None], (32, 16, 128))], axis=1
-    )
-    got = lax.all_to_all(send, PLANE, 0, 0).reshape(2, 16, 48, 128)
-    table = got[:, :, 32:, :].transpose(1, 0, 2, 3).reshape(16, 32, 128)
-    rows = got[:, :, :32, :].reshape(2, 16, 4, 8, 4, 32)
-    projected = jnp.einsum("hgkjay,gyq->hjakq", rows, table, precision=HIGHEST).reshape(64, 512)
-
-    below, above = [projected], [projected]
-    from_above = [(i, (i - 1) % 16) for i in range(16)]
-    from_below = [(i, (i + 1) % 16) for i in range(16)]
-    for _ in range(4):
-        above.append(lax.ppermute(above[-1], "z", from_above))
-        below.append(lax.ppermute(below[-1], "z", from_below))
-    blocks = below[:0:-1] + above
-    tied, *_ = lax.optimization_barrier((projected, below[-1], above[-1]))
+    got = lax.all_to_all(send.reshape(32, 48, 128), PLANE, 0, 0)
+    projected = projected_rows(got.reshape(32 * 48, 128))
+
+    def from_z(block, distance):
+        return lax.ppermute(block, "z", [(i, (i - distance) % 16) for i in range(16)])
+
+    near = {d: from_z(projected, d) for d in (2, -2, 1, -1)}
+    for sign in (1, -1):
+        pair = from_z(jnp.concatenate([near[sign], near[2 * sign]], axis=0), 2 * sign)
+        near[3 * sign], near[4 * sign] = pair[:64], pair[64:]
+    near[0] = projected
+    blocks = [near[d] for d in range(-4, 5)]
+    tied, *_ = lax.optimization_barrier((projected, near[4], near[-4]))
     every = lax.all_gather(tied, "z").reshape(1024, 512)
 
     part = lax.all_to_all(strips(z, blocks), PLANE, 0, 0).sum(0)
@@ -249,7 +349,8 @@
     mine = mine.reshape(16 * PART, 128)
     other = lax.ppermute(mine, "c", [(0, 1), (1, 0)])
 
-    x_factor, core = sweeps(jnp.stack([z, h, c]), mine, other, every)
+    x_factor, cols = sweeps(jnp.stack([z, h, c]), mine, other)
+    core = core_rows(cols, every)
     core = core.reshape(2, 4, 4, 16, 8).transpose(0, 3, 1, 2, 4).reshape(32, 1, 128)
     core = lax.all_to_all(core, PLANE, 0, 0).reshape(32, 4, 4, 8)
     core = core.transpose(1, 3, 0, 2).reshape(4, 1024)

time: 217 us -> 201 us (0.926)
  starting transfers between devices: 50.8 us -> 43.9 us
  matrix products: 6.31 us -> 0 us
  local copies, waits for them, and re-layouts: 7.95 us -> 3.61 us
  blocking collectives: 75.2 us -> 78.4 us
  waiting for transfers between devices: 16.4 us -> 19.2 us
    pallas_call x1, Pallas kernels: 40.7 us -> 30.7 us  [sweeps(): pl.pallas_call(sweeps_kernel, out_shape=(jax.ShapeDtypeStruct((32, RX), j...]
    ppermute x8 -> x6, starting transfers between devices: 32.7 us -> 24.3 us  [from_z(): lax.ppermute(block, 'z', [(i, (i - distance) % 16) for i in range(16)])]
    pallas_call x0 -> x3, Pallas kernels: none -> 7.14 us  [the longest x1 5.06 us: reduced_blocks(): pl.pallas_call(reduced_kernel, out_shape=jax.ShapeDtypeStruct((32 * 48, 1...]
    dot_general x2 -> x0, matrix products: 6.31 us -> none  [the longest x1 3.7 us: local(): lax.dot_general(kronecker, flow_field.reshape(1024, NZ * NV), (((0,), (1,...]
    all_gather x1, blocking collectives: 21.1 us -> 26.1 us  [local(): line = lax.all_gather(part, 'z')]
    ppermute x8 -> x6, waiting for transfers between devices: 5.3 us -> 8.18 us  [from_z(): lax.ppermute(block, 'z', [(i, (i - distance) % 16) for i in range(16)])]
    all_to_all x1, blocking collectives: 12.5 us -> 10.2 us  [local(): core = lax.all_to_all(core, PLANE, 0, 0).reshape(32, 4, 4, 8)]
    convert_element_type x1 -> x0, local copies, waits for them, and re-layouts: 2.26 us -> none  [kronecker_table(): return table.reshape(NZ * NV, RZ * RV).astype(jnp.bfloat16)]
  transfers between devices with their start and end apart: 11 -> 9, of which waited for: 4 -> 5; matrix products, arithmetic and copies ran while one was open for 0% -> 0% of each run, Pallas kernels for 1% -> 17%
where the time goes in v3:
time: 201 us; the launch traced here: 200 us
  blocking collectives  78.4 us (39%)
  starting transfers between devices  43.9 us (22%)
  Pallas kernels  40.9 us (20%)
  waiting for transfers between devices  19.2 us (10%)
  between operations  14.3 us (7%)
  local copies, waits for them, and re-layouts  3.61 us (2%)
    pallas_call x1, Pallas kernels, sweeps(): pl.pallas_call(sweeps_kernel, out_shape=(jax.ShapeDtypeStruct((32, RX), j...  30.7 us
    all_gather x1, blocking collectives, local(): line = lax.all_gather(part, 'z')  26.1 us
    all_to_all x1, blocking collectives, local(): got = lax.all_to_all(send.reshape(32, 48, 128), PLANE, 0, 0)  24.6 us
    ppermute x6, starting transfers between devices, from_z(): lax.ppermute(block, 'z', [(i, (i - distance) % 16) for i in range(16)])  24.3 us
    all_to_all x1, blocking collectives, local(): lax.all_to_all(jnp.broadcast_to(line[None], (16, PART, 128)), XY, 0, 0)  17.6 us
    all_to_all x1, blocking collectives, local(): core = lax.all_to_all(core, PLANE, 0, 0).reshape(32, 4, 4, 8)  10.2 us
    all_to_all x1, starting transfers between devices, local(): part = lax.all_to_all(strips(z, blocks), PLANE, 0, 0).sum(0)  10 us
    ppermute x1, starting transfers between devices, local(): other = lax.ppermute(mine, 'c', [(0, 1), (1, 0)])  9.49 us
  transfers between devices with their start and end apart: 9, of which 5 were waited for; matrix products, arithmetic and copies ran while one was open for 0% of the time, Pallas kernels for 17%

profile of v3, /device:TPU:1, one launch (start us, length us, event | category | flops | bytes accessed | tf_op | source)
XLA Modules:
  0.0 200.4 jit_solution(14739174738115853299)
XLA Ops:
  7.2 0.0 copy-start
  7.2 0.0 all-gather.4.cloned.1.call-start
  7.2 5.1 %reduced_blocks.1 = f32[1536,128]{1,0:T(8,128)} custom-call(s32[1]{0:T(128)} %bitcast.1.where_ref, bf16[1024,2048]{1,0:T(8,128)(2,1)} %bitcast.26, bf16[32,128]{1,0:T(8,128)(2,1)} %y_ref.1, bf16[16,64]{1,0:T(8,128)(2,1)} %bitcast.36, bf16[8,32]{1,0:T(8,128)(2,1)} %bitcast.37), custom_call_target="tpu_custom_call" | custom-call | tf_op jit(solution)/shard_map/reduced_blocks/pallas_call | solution.py:57
  12.3 24.6 %all_to_all.20 = f32[32,48,128]{2,1,0:T(8,128)S(1)} all-to-all(f32[32,48,128]{2,1,0:T(8,128)} %bitcast.27), channel_id=1, replica_groups=mesh['z'=16,'h'=2,'y'=4,'l'=2,'c'=2] {'h','y','l','c'}, dimensions={0} | all-to-all | bytes 1572864 | tf_op jit(solution)/shard_map/all_to_all | solution.py:325
  36.8 1.1 projected_rows.1.refs_4_
  37.9 9.2 %collective-permute-start.3 = (f32[64,512]{1,0:T(8,128)}, f32[64,512]{1,0:T(8,128)S(1)}, u32[]{:S(2)}, u32[]{:S(2)}) collective-permute-start(f32[64,512]{1,0:T(8,128)} %projected_rows.1.refs_4_), channel_id=1, source_target_pairs={{0,480},{32,0},{64,32},{96,64},{128,96},{160,128},{192,160},{224,1... | collective-permute-start | bytes 393224 | tf_op jit(solution)/shard_map/ppermute | solution.py:329
  47.1 3.1 %collective-permute-start.4 = (f32[64,512]{1,0:T(8,128)}, f32[64,512]{1,0:T(8,128)S(1)}, u32[]{:S(2)}, u32[]{:S(2)}) collective-permute-start(f32[64,512]{1,0:T(8,128)} %projected_rows.1.refs_4_), channel_id=1, source_target_pairs={{0,448},{32,480},{64,0},{96,32},{128,64},{160,96},{192,128},{224,1... | collective-permute-start | bytes 393224 | tf_op jit(solution)/shard_map/ppermute | solution.py:329
  50.2 2.6 %collective-permute-start = (f32[64,512]{1,0:T(8,128)}, f32[64,512]{1,0:T(8,128)S(1)}, u32[]{:S(2)}, u32[]{:S(2)}) collective-permute-start(f32[64,512]{1,0:T(8,128)} %projected_rows.1.refs_4_), channel_id=1, source_target_pairs={{0,32},{32,64},{64,96},{96,128},{128,160},{160,192},{192,224},{224... | collective-permute-start | bytes 393224 | tf_op jit(solution)/shard_map/ppermute | solution.py:329
  52.8 2.4 %collective-permute-start.1 = (f32[64,512]{1,0:T(8,128)}, f32[64,512]{1,0:T(8,128)S(1)}, u32[]{:S(2)}, u32[]{:S(2)}) collective-permute-start(f32[64,512]{1,0:T(8,128)} %projected_rows.1.refs_4_), channel_id=1, source_target_pairs={{0,64},{32,96},{64,128},{96,160},{128,192},{160,224},{192,256},{22... | collective-permute-start | bytes 393224 | tf_op jit(solution)/shard_map/ppermute | solution.py:329
  55.2 0.0 collective-permute-done.3.refs_5_
  55.2 0.0 collective-permute-done.4.refs_6_
  55.3 5.0 %collective-permute-start.5 = (f32[128,512]{1,0:T(8,128)S(1)}, f32[128,512]{1,0:T(8,128)S(1)}, u32[]{:S(2)}, u32[]{:S(2)}) collective-permute-start(f32[128,512]{1,0:T(8,128)S(1)} %pad_maximum_fusion.1), channel_id=1, source_target_pairs={{0,448},{32,480},{64,0},{96,32},{128,64},{160,96},{192,128},{224,1... | collective-permute-start | bytes 786440 | tf_op jit(solution)/shard_map/ppermute | solution.py:329
  60.3 0.0 collective-permute-done.refs_3_
  60.3 1.0 collective-permute-done.1.refs_2_
  61.3 2.1 %collective-permute-start.2 = (f32[128,512]{1,0:T(8,128)S(1)}, f32[128,512]{1,0:T(8,128)S(1)}, u32[]{:S(2)}, u32[]{:S(2)}) collective-permute-start(f32[128,512]{1,0:T(8,128)S(1)} %pad_maximum_fusion), channel_id=1, source_target_pairs={{0,64},{32,96},{64,128},{96,160},{128,192},{160,224},{192,256},{22... | collective-permute-start | bytes 786440 | tf_op jit(solution)/shard_map/ppermute | solution.py:329
  63.4 5.9 %collective-permute-done.5 = f32[128,512]{1,0:T(8,128)S(1)} collective-permute-done((f32[128,512]{1,0:T(8,128)S(1)}, f32[128,512]{1,0:T(8,128)S(1)}, u32[]{:S(2)}, u32[]{:S(2)}) %collective-permute-start.5) | collective-permute-done | bytes 262176 | tf_op jit(solution)/shard_map/ppermute | solution.py:329
  69.3 1.3 collective-permute-done.2
  70.6 0.0 all-gather.4.cloned.1.call-update
  70.6 3.0 %strips.1 = f32[32,16,128]{2,1,0:T(8,128)} custom-call(s32[1]{0:T(128)} %bitcast.where_ref, f32[64,512]{1,0:T(8,128)S(1)} %get-tuple-element.11.refs_0_, f32[64,512]{1,0:T(8,128)S(1)} %get-tuple-element.10.refs_1_, f32[64,512]{1,0:T(8,128)S(1)} %collective-permute-done.1.refs_2_, f32[64,512]{1,0:T(8,128)S(1)} %collective-permute-done.refs_3_, ...), custom_call_target="tpu_custom_call" | custom-call | tf_op jit(solution)/shard_map/strips/pallas_call | solution.py:131
  73.7 10.0 %all-to-all-start.1 = ((f32[32,16,128]{2,1,0:T(8,128)}), f32[32,16,128]{2,1,0:T(8,128)S(1)}, u32[]{:S(2)}, u32[]{:S(2)}) async-start(f32[32,16,128]{2,1,0:T(8,128)} %strips.1), calls=%async_computation.1 | async-start | bytes 524288 | tf_op jit(solution)/shard_map/all_to_all | solution.py:340
  83.7 0.1 pad.5.clone
  83.8 0.0 copy-done
  83.8 8.5 %all-to-all-done.1 = f32[32,16,128]{2,1,0:T(8,128)S(1)} async-done(((f32[32,16,128]{2,1,0:T(8,128)}), f32[32,16,128]{2,1,0:T(8,128)S(1)}, u32[]{:S(2)}, u32[]{:S(2)}) %all-to-all-start.1) | async-done | bytes 262176 | tf_op jit(solution)/shard_map/all_to_all | solution.py:340
  92.3 0.1 maximum_maximum_fusion
  92.4 26.1 %all-gather = f32[256,128]{1,0:T(8,128)S(1)} all-gather(f32[16,128]{1,0:T(8,128)S(1)} %maximum_maximum_fusion), channel_id=2, replica_groups=mesh['z'=16,'h'=2,'y'=4,'l'=2,'c'=2] {'z'}, dimensions={0}, use_global_device_ids=true | all-gather | bytes 139264 | tf_op jit(solution)/shard_map/all_gather | solution.py:344
  118.5 0.1 broadcast_in_dim.10
  118.6 17.6 %all_to_all.21 = f32[16,168,128]{2,1,0:T(8,128)S(1)} all-to-all(f32[16,168,128]{2,1,0:T(8,128)S(1)} %broadcast_in_dim.10), channel_id=1, replica_groups=mesh['z'=16,'h'=2,'y'=4,'l'=2,'c'=2] {'h','y','l'}, dimensions={0} | all-to-all | bytes 2752512 | tf_op jit(solution)/shard_map/all_to_all | solution.py:348
  136.2 9.5 %collective-permute-start.6 = (f32[2688,128]{1,0:T(8,128)S(1)}, f32[2688,128]{1,0:T(8,128)S(1)}, u32[]{:S(2)}, u32[]{:S(2)}) collective-permute-start(f32[2688,128]{1,0:T(8,128)S(1)} %bitcast.23), channel_id=1, source_target_pairs={{0,1},{1,0},{2,3},{3,2},{4,5},{5,4},{6,7},{7,6},{8,9},{9,8},{10,11... | collective-permute-start | bytes 4128776 | tf_op jit(solution)/shard_map/ppermute | solution.py:350
  145.7 0.1 pad_add_fusion.where_ref
  145.8 2.5 %collective-permute-done.6.other = f32[2688,128]{1,0:T(8,128)S(1)} collective-permute-done((f32[2688,128]{1,0:T(8,128)S(1)}, f32[2688,128]{1,0:T(8,128)S(1)}, u32[]{:S(2)}, u32[]{:S(2)}) %collective-permute-start.6) | collective-permute-done | bytes 1376288 | tf_op jit(solution)/shard_map/ppermute | solution.py:350
  148.2 30.7 %sweeps.1 = (f32[32,128]{1,0:T(8,128)}, f32[8,1024]{1,0:T(8,128)S(1)}) custom-call(s32[3]{0:T(128)S(1)} %pad_add_fusion.where_ref, f32[2688,128]{1,0:T(8,128)S(1)} %bitcast.24, f32[2688,128]{1,0:T(8,128)S(1)} %collective-permute-done.6.other), custom_call_target="tpu_custom_call" | custom-call | tf_op jit(solution)/shard_map/sweeps/pallas_call | solution.py:293
  179.0 0.0 all-gather.4.cloned.1.call-done.every_ref
  179.0 0.0 copy-start.1
  179.0 1.6 copy-done.1
  180.6 1.0 core_rows.1
  181.6 0.2 reshape.47
  181.8 0.2 copy.10
  181.9 0.1 reshape.48
  182.1 0.1 copy.11
  182.1 10.2 %all_to_all.22 = f32[32,1,128]{2,1,0:T(1,128)S(1)} all-to-all(f32[32,1,128]{2,1,0:T(1,128)S(1)} %copy.11), channel_id=1, replica_groups=mesh['z'=16,'h'=2,'y'=4,'l'=2,'c'=2] {'h','y','l','c'}, dimensions={0} | all-to-all | bytes 32768 | tf_op jit(solution)/shard_map/all_to_all | solution.py:355
  192.3 0.1 copy.12
  192.4 0.3 copy.13
  192.7 0.9 reshape.50
  (11 shorter events, 0.1 us)
Async XLA Ops:
  7.2 76.6 %copy-start = (f32[32,128]{1,0:T(8,128)S(1)}, f32[32,128]{1,0:T(8,128)}, u32[]{:S(2)}) copy-start(f32[32,128]{1,0:T(8,128)} %param.9) | copy-start | bytes 49156
  7.2 171.8 %all-gather.4.cloned.1.call-start = ((), (), s32[]{:S(2)}) async-start(), calls=%async_computation.4 | async-start | bytes 2228224 | tf_op jit(solution)/shard_map/all_gather | solution.py:338
  37.9 17.3 %collective-permute-start.3 = (f32[64,512]{1,0:T(8,128)}, f32[64,512]{1,0:T(8,128)S(1)}, u32[]{:S(2)}, u32[]{:S(2)}) collective-permute-start(f32[64,512]{1,0:T(8,128)} %projected_rows.1.refs_4_), channel_id=1, source_target_pairs={{0,480},{32,0},{64,32},{96,64},{128,96},{160,128},{192,160},{224,1... | collective-permute-start | bytes 393224 | tf_op jit(solution)/shard_map/ppermute | solution.py:329
  47.1 8.1 %collective-permute-start.4 = (f32[64,512]{1,0:T(8,128)}, f32[64,512]{1,0:T(8,128)S(1)}, u32[]{:S(2)}, u32[]{:S(2)}) collective-permute-start(f32[64,512]{1,0:T(8,128)} %projected_rows.1.refs_4_), channel_id=1, source_target_pairs={{0,448},{32,480},{64,0},{96,32},{128,64},{160,96},{192,128},{224,1... | collective-permute-start | bytes 393224 | tf_op jit(solution)/shard_map/ppermute | solution.py:329
  50.2 10.1 %collective-permute-start = (f32[64,512]{1,0:T(8,128)}, f32[64,512]{1,0:T(8,128)S(1)}, u32[]{:S(2)}, u32[]{:S(2)}) collective-permute-start(f32[64,512]{1,0:T(8,128)} %projected_rows.1.refs_4_), channel_id=1, source_target_pairs={{0,32},{32,64},{64,96},{96,128},{128,160},{160,192},{192,224},{224... | collective-permute-start | bytes 393224 | tf_op jit(solution)/shard_map/ppermute | solution.py:329
  52.8 8.5 %collective-permute-start.1 = (f32[64,512]{1,0:T(8,128)}, f32[64,512]{1,0:T(8,128)S(1)}, u32[]{:S(2)}, u32[]{:S(2)}) collective-permute-start(f32[64,512]{1,0:T(8,128)} %projected_rows.1.refs_4_), channel_id=1, source_target_pairs={{0,64},{32,96},{64,128},{96,160},{128,192},{160,224},{192,256},{22... | collective-permute-start | bytes 393224 | tf_op jit(solution)/shard_map/ppermute | solution.py:329
  55.3 14.0 %collective-permute-start.5 = (f32[128,512]{1,0:T(8,128)S(1)}, f32[128,512]{1,0:T(8,128)S(1)}, u32[]{:S(2)}, u32[]{:S(2)}) collective-permute-start(f32[128,512]{1,0:T(8,128)S(1)} %pad_maximum_fusion.1), channel_id=1, source_target_pairs={{0,448},{32,480},{64,0},{96,32},{128,64},{160,96},{192,128},{224,1... | collective-permute-start | bytes 786440 | tf_op jit(solution)/shard_map/ppermute | solution.py:329
  61.3 9.2 %collective-permute-start.2 = (f32[128,512]{1,0:T(8,128)S(1)}, f32[128,512]{1,0:T(8,128)S(1)}, u32[]{:S(2)}, u32[]{:S(2)}) collective-permute-start(f32[128,512]{1,0:T(8,128)S(1)} %pad_maximum_fusion), channel_id=1, source_target_pairs={{0,64},{32,96},{64,128},{96,160},{128,192},{160,224},{192,256},{22... | collective-permute-start | bytes 786440 | tf_op jit(solution)/shard_map/ppermute | solution.py:329
  73.7 18.6 %all-to-all-start.1 = ((f32[32,16,128]{2,1,0:T(8,128)}), f32[32,16,128]{2,1,0:T(8,128)S(1)}, u32[]{:S(2)}, u32[]{:S(2)}) async-start(f32[32,16,128]{2,1,0:T(8,128)} %strips.1), calls=%async_computation.1 | async-start | bytes 524288 | tf_op jit(solution)/shard_map/all_to_all | solution.py:340
  136.2 12.0 %collective-permute-start.6 = (f32[2688,128]{1,0:T(8,128)S(1)}, f32[2688,128]{1,0:T(8,128)S(1)}, u32[]{:S(2)}, u32[]{:S(2)}) collective-permute-start(f32[2688,128]{1,0:T(8,128)S(1)} %bitcast.23), channel_id=1, source_target_pairs={{0,1},{1,0},{2,3},{3,2},{4,5},{5,4},{6,7},{7,6},{8,9},{9,8},{10,11... | collective-permute-start | bytes 4128776 | tf_op jit(solution)/shard_map/ppermute | solution.py:350
  179.0 1.6 copy-start.1
Sparse Core Ops, SparseCore 0:
  70.8 66.0 all-gather.3

commit v4 on v3

--- a/solution.py
+++ b/solution.py
@@ -71,7 +71,7 @@
     )(where, flow, y_factor, z_factor, v_factor)
 
 
-def projected_kernel(got, out_ref, ordered):
+def projected_kernel(got, out_ref, own_ref, ordered):
     quarter = lax.broadcasted_iota(jnp.int32, (64, 128), 1) // 32
     total = jnp.zeros((256, 128), jnp.float32)
     for gy in range(0, 16, 2):
@@ -94,14 +94,15 @@
                 ordered[pl.ds(k * 64 + h * 32 + a, 8, stride=4), :] = total[base : base + 8, :]
     for k in range(4):
         out_ref[:, k * 128 : k * 128 + 128] = ordered[k * 64 : k * 64 + 64, :]
+        own_ref[:, k * 128 : k * 128 + 128] = ordered[k * 64 : k * 64 + 64, :]
 
 
 def projected_rows(got):
     return pl.pallas_call(
         projected_kernel,
-        out_shape=jax.ShapeDtypeStruct((64, 512), jnp.float32),
+        out_shape=(jax.ShapeDtypeStruct((64, 512), jnp.float32),) * 2,
         in_specs=[pl.BlockSpec(memory_space=pltpu.VMEM)],
-        out_specs=pl.BlockSpec(memory_space=pltpu.VMEM),
+        out_specs=[pl.BlockSpec(memory_space=pltpu.VMEM)] * 2,
         scratch_shapes=[pltpu.VMEM((256, 128), jnp.float32)],
         compiler_params=pltpu.CompilerParams(vmem_limit_bytes=16 * 1024 * 1024),
         name="projected_rows",
@@ -134,7 +135,7 @@
         in_specs=[pl.BlockSpec(memory_space=pltpu.SMEM)]
         + [pl.BlockSpec(memory_space=pltpu.VMEM)] * 9,
         out_specs=pl.BlockSpec(memory_space=pltpu.VMEM),
-        compiler_params=pltpu.CompilerParams(vmem_limit_bytes=24 * 1024 * 1024),
+        compiler_params=pltpu.CompilerParams(vmem_limit_bytes=16 * 1024 * 1024),
         name="strips",
     )(z.reshape(1), *blocks)
 
@@ -143,6 +144,9 @@
     full = (8, 128)
     sub = lax.broadcasted_iota(jnp.int32, full, 0)
     lane = lax.broadcasted_iota(jnp.int32, full, 1)
+    left = [correlation[8 * v : 8 * v + 8, :] for v in range(16)]
+    right = [jnp.where(lane == sub + 8 * v, 1.0, 0.0) for v in range(16)]
+    done = []
 
     def row(x, i):
         return jnp.broadcast_to(x[i : i + 1, :], full)
@@ -150,56 +154,40 @@
     def column(x, j):
         return jnp.broadcast_to(x[:, j : j + 1], full)
 
-    def total(t):
-        return ((t[0] + t[1]) + (t[2] + t[3])) + ((t[4] + t[5]) + (t[6] + t[7]))
-
-    left = [correlation[8 * v : 8 * v + 8, :] for v in range(16)]
-    eye = [lane == sub + 8 * v for v in range(16)]
-    on = [jnp.where(eye[v], left[v], 0.0) for v in range(16)]
-    acc = on[0]
-    for v in range(1, 16):
-        acc = acc + on[v]
-    across = lax.rsqrt(jnp.broadcast_to(jnp.sum(acc, axis=0, keepdims=True), full))
-    down = [lax.rsqrt(jnp.broadcast_to(jnp.sum(on[v], axis=1, keepdims=True), full)) for v in range(16)]
-    left = [left[v] * across * down[v] for v in range(16)]
-    right = [jnp.where(eye[v], across, 0.0) for v in range(16)]
-    done = []
     for v in range(16):
         small = [column(left[v], 8 * v + i) for i in range(8)]
         rest, made = left[v], right[v]
         finished = jnp.zeros(full, jnp.float32)
-        for i in (0, 2, 4, 6):
-            j = i + 1
-            a, b, d = row(small[i], i), row(small[i], j), row(small[j], j)
-            inverse = 1.0 / (a * d - b * b)
-            ia, ib, id_ = d * inverse, b * inverse, a * inverse
-            at_i, at_j = sub == i, sub == j
-            here = jnp.logical_or(at_i, at_j)
-            share_i = jnp.where(at_i, -ia, jnp.where(at_j, ib, small[i] * ia - small[j] * ib))
-            share_j = jnp.where(at_i, ib, jnp.where(at_j, -id_, small[j] * id_ - small[i] * ib))
-            made_i, made_j = row(made, i), row(made, j)
-            root = lax.rsqrt(a)
-            root = root * (1.5 - 0.5 * a * root * root)
-            ratio = b * root * root
-            left_over = d - b * ratio
-            second = lax.rsqrt(left_over)
-            second = second * (1.5 - 0.5 * left_over * second * second)
-            finished = jnp.where(at_i, made_i * root, jnp.where(at_j, (made_j - ratio * made_i) * second, finished))
-            def less(x, x_i, x_j):
-                return jnp.where(here, 0.0, x) - (share_i * x_i + share_j * x_j)
-            made = less(made, made_i, made_j)
+        for i in range(8):
+            pivot = row(small[i], i)
+            inverse = 1.0 / pivot
+            here = sub == i
+            share = jnp.where(here, -inverse, small[i] * inverse)
+            made_row = row(made, i)
+            root = lax.rsqrt(pivot)
+            root = root * (1.5 - 0.5 * pivot * root * root)
+            finished = jnp.where(here, made_row * root, finished)
+            made = jnp.where(here, 0.0, made) - share * made_row
             if v < 15:
-                rest = less(rest, row(rest, i), row(rest, j))
-            for k in range(i + 2, 8):
-                small[k] = less(small[k], row(small[k], i), row(small[k], j))
+                rest = jnp.where(here, 0.0, rest) - share * row(rest, i)
+            for k in range(i + 1, 8):
+                small[k] = jnp.where(here, 0.0, small[k]) - share * row(small[k], i)
         done.append(finished)
         if v < 15:
             rest_rows = [row(rest, i) for i in range(8)]
             made_rows = [row(made, i) for i in range(8)]
             for w in range(v + 1, 16):
                 shares = [column(left[w], 8 * v + i) for i in range(8)]
-                left[w] = left[w] - total([shares[i] * rest_rows[i] for i in range(8)])
-                right[w] = right[w] - total([shares[i] * made_rows[i] for i in range(8)])
+                taken = [shares[i] * rest_rows[i] for i in range(8)]
+                left[w] = left[w] - (
+                    ((taken[0] + taken[1]) + (taken[2] + taken[3]))
+                    + ((taken[4] + taken[5]) + (taken[6] + taken[7]))
+                )
+                taken = [shares[i] * made_rows[i] for i in range(8)]
+                right[w] = right[w] - (
+                    ((taken[0] + taken[1]) + (taken[2] + taken[3]))
+                    + ((taken[4] + taken[5]) + (taken[6] + taken[7]))
+                )
     return jnp.concatenate(done, axis=0)
 
 
@@ -323,7 +311,7 @@
         h.reshape(1), flow_field.reshape(1024, NZ * NV), y_factor, z_factor.T, v_factor.T
     )
     got = lax.all_to_all(send.reshape(32, 48, 128), PLANE, 0, 0)
-    projected = projected_rows(got.reshape(32 * 48, 128))
+    projected, own = projected_rows(got.reshape(32 * 48, 128))
 
     def from_z(block, distance):
         return lax.ppermute(block, "z", [(i, (i - distance) % 16) for i in range(16)])
@@ -334,14 +322,15 @@
         near[3 * sign], near[4 * sign] = pair[:64], pair[64:]
     near[0] = projected
     blocks = [near[d] for d in range(-4, 5)]
-    tied, *_ = lax.optimization_barrier((projected, near[4], near[-4]))
-    every = lax.all_gather(tied, "z").reshape(1024, 512)
+
+    own, *_ = lax.optimization_barrier((own, near[4], near[-4]))
+    every = lax.all_gather(own, "z").reshape(1024, 512)
 
     part = lax.all_to_all(strips(z, blocks), PLANE, 0, 0).sum(0)
     gy = (lax.axis_index("y") * 4 + lax.axis_index("l") * 2 + c).astype(jnp.int32)
     start = lax.dynamic_slice_in_dim(x_start, 2 * gy, 2, 0)
     part = jnp.concatenate([part[:9], start, jnp.zeros((5, 128), jnp.float32)], axis=0)
-    line = lax.all_gather(part, "z")
+    line = lax.all_to_all(jnp.broadcast_to(part[None], (16, 16, 128)), "z", 0, 0)
     line = jnp.concatenate(
         [line[:, :8].reshape(128, 128), line[:8, 8], line[:, 9:11].reshape(32, 128)], axis=0
     )

time: 201 us -> 195 us (0.970)
  starting transfers between devices: 43.9 us -> 41.1 us
    all_gather x1 -> x0, blocking collectives: 26.1 us -> none  [local(): line = lax.all_gather(part, 'z')]
    all_to_all x0 -> x1, blocking collectives: none -> 22 us  [local(): lax.all_to_all(jnp.broadcast_to(part[None], (16, 16, 128)), 'z', 0, 0)]
    ppermute x1, starting transfers between devices: 9.49 us -> 6.69 us  [local(): other = lax.ppermute(mine, 'c', [(0, 1), (1, 0)])]
    all_to_all x1, blocking collectives: 17.6 us -> 19.7 us  [local(): lax.all_to_all(jnp.broadcast_to(line[None], (16, PART, 128)), XY, 0, 0)]
  transfers between devices with their start and end apart: 9 -> 9, of which waited for: 5 -> 5; matrix products, arithmetic and copies ran while one was open for 0% -> 0% of each run, Pallas kernels for 17% -> 15%
where the time goes in v4:
time: 195 us; the launch traced here: 193 us
  blocking collectives  76.4 us (39%)
  starting transfers between devices  41.1 us (21%)
  Pallas kernels  39 us (20%)
  waiting for transfers between devices  18.9 us (10%)
  between operations  14.3 us (7%)
  local copies, waits for them, and re-layouts  3.63 us (2%)
    pallas_call x1, Pallas kernels, sweeps(): pl.pallas_call(sweeps_kernel, out_shape=(jax.ShapeDtypeStruct((32, RX), j...  29.7 us
    all_to_all x1, blocking collectives, local(): got = lax.all_to_all(send.reshape(32, 48, 128), PLANE, 0, 0)  24.6 us
    ppermute x6, starting transfers between devices, from_z(): lax.ppermute(block, 'z', [(i, (i - distance) % 16) for i in range(16)])  24.3 us
    all_to_all x1, blocking collectives, local(): lax.all_to_all(jnp.broadcast_to(part[None], (16, 16, 128)), 'z', 0, 0)  22 us
    all_to_all x1, blocking collectives, local(): lax.all_to_all(jnp.broadcast_to(line[None], (16, PART, 128)), XY, 0, 0)  19.7 us
    all_to_all x1, blocking collectives, local(): core = lax.all_to_all(core, PLANE, 0, 0).reshape(32, 4, 4, 8)  10.2 us
    all_to_all x1, starting transfers between devices, local(): part = lax.all_to_all(strips(z, blocks), PLANE, 0, 0).sum(0)  10 us
    ppermute x6, waiting for transfers between devices, from_z(): lax.ppermute(block, 'z', [(i, (i - distance) % 16) for i in range(16)])  7.97 us
  transfers between devices with their start and end apart: 9, of which 5 were waited for; matrix products, arithmetic and copies ran while one was open for 0% of the time, Pallas kernels for 15%

profile of v4, /device:TPU:1, one launch (start us, length us, event | category | flops | bytes accessed | tf_op | source)
XLA Modules:
  0.0 193.5 jit_solution(9755357043284484194)
XLA Ops:
  7.2 0.0 copy-start
  7.2 5.0 %reduced_blocks.1 = f32[1536,128]{1,0:T(8,128)} custom-call(s32[1]{0:T(128)} %bitcast.1.where_ref, bf16[1024,2048]{1,0:T(8,128)(2,1)} %bitcast.27, bf16[32,128]{1,0:T(8,128)(2,1)} %y_ref.1, bf16[16,64]{1,0:T(8,128)(2,1)} %bitcast.34, bf16[8,32]{1,0:T(8,128)(2,1)} %bitcast.35), custom_call_target="tpu_custom_call" | custom-call | tf_op jit(solution)/shard_map/reduced_blocks/pallas_call | solution.py:57
  12.2 24.6 %all_to_all.25 = f32[32,48,128]{2,1,0:T(8,128)S(1)} all-to-all(f32[32,48,128]{2,1,0:T(8,128)} %bitcast.28), channel_id=1, replica_groups=mesh['z'=16,'h'=2,'y'=4,'l'=2,'c'=2] {'h','y','l','c'}, dimensions={0} | all-to-all | bytes 1572864 | tf_op jit(solution)/shard_map/all_to_all | solution.py:313
  36.8 1.1 projected_rows.1
  37.9 9.2 %collective-permute-start.3 = (f32[64,512]{1,0:T(8,128)S(1)}, f32[64,512]{1,0:T(8,128)S(1)}, u32[]{:S(2)}, u32[]{:S(2)}) collective-permute-start(f32[64,512]{1,0:T(8,128)S(1)} %get-tuple-element.7.refs_4_), channel_id=1, source_target_pairs={{0,480},{32,0},{64,32},{96,64},{128,96},{160,128},{192,160},{224,1... | collective-permute-start | bytes 393224 | tf_op jit(solution)/shard_map/ppermute | solution.py:317
  47.0 3.1 %collective-permute-start.4 = (f32[64,512]{1,0:T(8,128)S(1)}, f32[64,512]{1,0:T(8,128)S(1)}, u32[]{:S(2)}, u32[]{:S(2)}) collective-permute-start(f32[64,512]{1,0:T(8,128)S(1)} %get-tuple-element.7.refs_4_), channel_id=1, source_target_pairs={{0,448},{32,480},{64,0},{96,32},{128,64},{160,96},{192,128},{224,1... | collective-permute-start | bytes 393224 | tf_op jit(solution)/shard_map/ppermute | solution.py:317
  50.1 2.6 %collective-permute-start = (f32[64,512]{1,0:T(8,128)S(1)}, f32[64,512]{1,0:T(8,128)S(1)}, u32[]{:S(2)}, u32[]{:S(2)}) collective-permute-start(f32[64,512]{1,0:T(8,128)S(1)} %get-tuple-element.7.refs_4_), channel_id=1, source_target_pairs={{0,32},{32,64},{64,96},{96,128},{128,160},{160,192},{192,224},{224... | collective-permute-start | bytes 393224 | tf_op jit(solution)/shard_map/ppermute | solution.py:317
  52.8 2.4 %collective-permute-start.1 = (f32[64,512]{1,0:T(8,128)S(1)}, f32[64,512]{1,0:T(8,128)S(1)}, u32[]{:S(2)}, u32[]{:S(2)}) collective-permute-start(f32[64,512]{1,0:T(8,128)S(1)} %get-tuple-element.7.refs_4_), channel_id=1, source_target_pairs={{0,64},{32,96},{64,128},{96,160},{128,192},{160,224},{192,256},{22... | collective-permute-start | bytes 393224 | tf_op jit(solution)/shard_map/ppermute | solution.py:317
  55.2 0.0 collective-permute-done.3.refs_5_
  55.2 0.0 collective-permute-done.4.refs_6_
  55.2 5.0 %collective-permute-start.5 = (f32[128,512]{1,0:T(8,128)S(1)}, f32[128,512]{1,0:T(8,128)S(1)}, u32[]{:S(2)}, u32[]{:S(2)}) collective-permute-start(f32[128,512]{1,0:T(8,128)S(1)} %pad_maximum_fusion.1), channel_id=1, source_target_pairs={{0,448},{32,480},{64,0},{96,32},{128,64},{160,96},{192,128},{224,1... | collective-permute-start | bytes 786440 | tf_op jit(solution)/shard_map/ppermute | solution.py:317
  60.2 0.0 collective-permute-done.refs_3_
  60.3 0.8 collective-permute-done.1.refs_2_
  61.1 2.1 %collective-permute-start.2 = (f32[128,512]{1,0:T(8,128)S(1)}, f32[128,512]{1,0:T(8,128)S(1)}, u32[]{:S(2)}, u32[]{:S(2)}) collective-permute-start(f32[128,512]{1,0:T(8,128)S(1)} %pad_maximum_fusion), channel_id=1, source_target_pairs={{0,64},{32,96},{64,128},{96,160},{128,192},{160,224},{192,256},{22... | collective-permute-start | bytes 786440 | tf_op jit(solution)/shard_map/ppermute | solution.py:317
  63.1 6.8 %collective-permute-done.5 = f32[128,512]{1,0:T(8,128)S(1)} collective-permute-done((f32[128,512]{1,0:T(8,128)S(1)}, f32[128,512]{1,0:T(8,128)S(1)}, u32[]{:S(2)}, u32[]{:S(2)}) %collective-permute-start.5) | collective-permute-done | bytes 262176 | tf_op jit(solution)/shard_map/ppermute | solution.py:317
  70.0 0.4 collective-permute-done.2
  70.3 2.1 %strips.1 = f32[32,16,128]{2,1,0:T(8,128)} custom-call(s32[1]{0:T(128)} %bitcast.where_ref, f32[64,512]{1,0:T(8,128)S(1)} %get-tuple-element.15.refs_0_, f32[64,512]{1,0:T(8,128)S(1)} %get-tuple-element.14.refs_1_, f32[64,512]{1,0:T(8,128)S(1)} %collective-permute-done.1.refs_2_, f32[64,512]{1,0:T(8,128)S(1)} %collective-permute-done.refs_3_, ...), custom_call_target="tpu_custom_call" | custom-call | tf_op jit(solution)/shard_map/strips/pallas_call | solution.py:132
  72.5 10.0 %all-to-all-start.1 = ((f32[32,16,128]{2,1,0:T(8,128)}), f32[32,16,128]{2,1,0:T(8,128)S(1)}, u32[]{:S(2)}, u32[]{:S(2)}) async-start(f32[32,16,128]{2,1,0:T(8,128)} %strips.1), calls=%async_computation.1 | async-start | bytes 524288 | tf_op jit(solution)/shard_map/all_to_all | solution.py:329
  82.5 0.0 all-gather.3.cloned.1.call-start
  82.5 0.7 all-gather.3.cloned.1.call-update
  83.2 0.1 pad.5.clone
  83.3 0.0 copy-done
  83.3 7.7 %all-to-all-done.1 = f32[32,16,128]{2,1,0:T(8,128)S(1)} async-done(((f32[32,16,128]{2,1,0:T(8,128)}), f32[32,16,128]{2,1,0:T(8,128)S(1)}, u32[]{:S(2)}, u32[]{:S(2)}) %all-to-all-start.1) | async-done | bytes 262176 | tf_op jit(solution)/shard_map/all_to_all | solution.py:329
  91.1 0.1 maximum_maximum_fusion
  91.2 22.0 %all_to_all.26 = f32[16,16,128]{2,1,0:T(8,128)S(1)} all-to-all(f32[16,16,128]{2,1,0:T(8,128)S(1)} %broadcast_in_dim.7), channel_id=1, replica_groups=mesh['z'=16,'h'=2,'y'=4,'l'=2,'c'=2] {'z'}, dimensions={0} | all-to-all | bytes 262144 | tf_op jit(solution)/shard_map/all_to_all | solution.py:333
  113.2 0.1 broadcast_in_dim.8
  113.3 19.7 %all_to_all.27 = f32[16,168,128]{2,1,0:T(8,128)S(1)} all-to-all(f32[16,168,128]{2,1,0:T(8,128)S(1)} %broadcast_in_dim.8), channel_id=1, replica_groups=mesh['z'=16,'h'=2,'y'=4,'l'=2,'c'=2] {'h','y','l'}, dimensions={0} | all-to-all | bytes 2752512 | tf_op jit(solution)/shard_map/all_to_all | solution.py:337
  133.0 6.7 %collective-permute-start.6 = (f32[2688,128]{1,0:T(8,128)S(1)}, f32[2688,128]{1,0:T(8,128)S(1)}, u32[]{:S(2)}, u32[]{:S(2)}) collective-permute-start(f32[2688,128]{1,0:T(8,128)S(1)} %bitcast.24), channel_id=1, source_target_pairs={{0,1},{1,0},{2,3},{3,2},{4,5},{5,4},{6,7},{7,6},{8,9},{9,8},{10,11... | collective-permute-start | bytes 4128776 | tf_op jit(solution)/shard_map/ppermute | solution.py:339
  139.7 0.1 pad_add_fusion.where_ref
  139.8 2.5 %collective-permute-done.6.other = f32[2688,128]{1,0:T(8,128)S(1)} collective-permute-done((f32[2688,128]{1,0:T(8,128)S(1)}, f32[2688,128]{1,0:T(8,128)S(1)}, u32[]{:S(2)}, u32[]{:S(2)}) %collective-permute-start.6) | collective-permute-done | bytes 1376288 | tf_op jit(solution)/shard_map/ppermute | solution.py:339
  142.3 29.7 %sweeps.1 = (f32[32,128]{1,0:T(8,128)}, f32[8,1024]{1,0:T(8,128)S(1)}) custom-call(s32[3]{0:T(128)S(1)} %pad_add_fusion.where_ref, f32[2688,128]{1,0:T(8,128)S(1)} %bitcast.25, f32[2688,128]{1,0:T(8,128)S(1)} %collective-permute-done.6.other), custom_call_target="tpu_custom_call" | custom-call | tf_op jit(solution)/shard_map/sweeps/pallas_call | solution.py:281
  172.0 0.0 all-gather.3.cloned.1.call-done.every_ref
  172.0 0.0 copy-start.1
  172.1 1.6 copy-done.1
  173.6 1.0 core_rows.1
  174.6 0.2 reshape.48
  174.8 0.2 copy.13
  175.0 0.1 reshape.49
  175.1 0.1 copy.14
  175.2 10.2 %all_to_all.28 = f32[32,1,128]{2,1,0:T(1,128)S(1)} all-to-all(f32[32,1,128]{2,1,0:T(1,128)S(1)} %copy.14), channel_id=1, replica_groups=mesh['z'=16,'h'=2,'y'=4,'l'=2,'c'=2] {'h','y','l','c'}, dimensions={0} | all-to-all | bytes 32768 | tf_op jit(solution)/shard_map/all_to_all | solution.py:344
  185.3 0.1 copy.15
  185.4 0.3 copy.16
  185.7 0.9 reshape.51
  (12 shorter events, 0.2 us)
Async XLA Ops:
  7.2 76.1 %copy-start = (f32[32,128]{1,0:T(8,128)S(1)}, f32[32,128]{1,0:T(8,128)}, u32[]{:S(2)}) copy-start(f32[32,128]{1,0:T(8,128)} %param.9) | copy-start | bytes 49156
  37.9 17.3 %collective-permute-start.3 = (f32[64,512]{1,0:T(8,128)S(1)}, f32[64,512]{1,0:T(8,128)S(1)}, u32[]{:S(2)}, u32[]{:S(2)}) collective-permute-start(f32[64,512]{1,0:T(8,128)S(1)} %get-tuple-element.7.refs_4_), channel_id=1, source_target_pairs={{0,480},{32,0},{64,32},{96,64},{128,96},{160,128},{192,160},{224,1... | collective-permute-start | bytes 393224 | tf_op jit(solution)/shard_map/ppermute | solution.py:317
  47.0 8.1 %collective-permute-start.4 = (f32[64,512]{1,0:T(8,128)S(1)}, f32[64,512]{1,0:T(8,128)S(1)}, u32[]{:S(2)}, u32[]{:S(2)}) collective-permute-start(f32[64,512]{1,0:T(8,128)S(1)} %get-tuple-element.7.refs_4_), channel_id=1, source_target_pairs={{0,448},{32,480},{64,0},{96,32},{128,64},{160,96},{192,128},{224,1... | collective-permute-start | bytes 393224 | tf_op jit(solution)/shard_map/ppermute | solution.py:317
  50.1 10.1 %collective-permute-start = (f32[64,512]{1,0:T(8,128)S(1)}, f32[64,512]{1,0:T(8,128)S(1)}, u32[]{:S(2)}, u32[]{:S(2)}) collective-permute-start(f32[64,512]{1,0:T(8,128)S(1)} %get-tuple-element.7.refs_4_), channel_id=1, source_target_pairs={{0,32},{32,64},{64,96},{96,128},{128,160},{160,192},{192,224},{224... | collective-permute-start | bytes 393224 | tf_op jit(solution)/shard_map/ppermute | solution.py:317
  52.8 8.3 %collective-permute-start.1 = (f32[64,512]{1,0:T(8,128)S(1)}, f32[64,512]{1,0:T(8,128)S(1)}, u32[]{:S(2)}, u32[]{:S(2)}) collective-permute-start(f32[64,512]{1,0:T(8,128)S(1)} %get-tuple-element.7.refs_4_), channel_id=1, source_target_pairs={{0,64},{32,96},{64,128},{96,160},{128,192},{160,224},{192,256},{22... | collective-permute-start | bytes 393224 | tf_op jit(solution)/shard_map/ppermute | solution.py:317
  55.2 14.7 %collective-permute-start.5 = (f32[128,512]{1,0:T(8,128)S(1)}, f32[128,512]{1,0:T(8,128)S(1)}, u32[]{:S(2)}, u32[]{:S(2)}) collective-permute-start(f32[128,512]{1,0:T(8,128)S(1)} %pad_maximum_fusion.1), channel_id=1, source_target_pairs={{0,448},{32,480},{64,0},{96,32},{128,64},{160,96},{192,128},{224,1... | collective-permute-start | bytes 786440 | tf_op jit(solution)/shard_map/ppermute | solution.py:317
  61.1 9.2 %collective-permute-start.2 = (f32[128,512]{1,0:T(8,128)S(1)}, f32[128,512]{1,0:T(8,128)S(1)}, u32[]{:S(2)}, u32[]{:S(2)}) collective-permute-start(f32[128,512]{1,0:T(8,128)S(1)} %pad_maximum_fusion), channel_id=1, source_target_pairs={{0,64},{32,96},{64,128},{96,160},{128,192},{160,224},{192,256},{22... | collective-permute-start | bytes 786440 | tf_op jit(solution)/shard_map/ppermute | solution.py:317
  72.5 18.6 %all-to-all-start.1 = ((f32[32,16,128]{2,1,0:T(8,128)}), f32[32,16,128]{2,1,0:T(8,128)S(1)}, u32[]{:S(2)}, u32[]{:S(2)}) async-start(f32[32,16,128]{2,1,0:T(8,128)} %strips.1), calls=%async_computation.1 | async-start | bytes 524288 | tf_op jit(solution)/shard_map/all_to_all | solution.py:329
  82.5 89.6 %all-gather.3.cloned.1.call-start = ((), (), s32[]{:S(2)}) async-start(), calls=%async_computation.5 | async-start | bytes 2228224 | tf_op jit(solution)/shard_map/all_gather | solution.py:327
  133.0 9.3 %collective-permute-start.6 = (f32[2688,128]{1,0:T(8,128)S(1)}, f32[2688,128]{1,0:T(8,128)S(1)}, u32[]{:S(2)}, u32[]{:S(2)}) collective-permute-start(f32[2688,128]{1,0:T(8,128)S(1)} %bitcast.24), channel_id=1, source_target_pairs={{0,1},{1,0},{2,3},{3,2},{4,5},{5,4},{6,7},{7,6},{8,9},{9,8},{10,11... | collective-permute-start | bytes 4128776 | tf_op jit(solution)/shard_map/ppermute | solution.py:339
  172.0 1.6 copy-start.1
Sparse Core Ops, SparseCore 0:
  85.4 68.5 all-gather.2

commit v5 on v4

--- a/solution.py
+++ b/solution.py
@@ -26,7 +26,7 @@
     return lax.dot_general(a, b, dims, precision=HIGHEST, preferred_element_type=jnp.float32)
 
 
-def reduced_kernel(where_ref, flow, y_ref, z_ref, v_ref, out_ref, held, table, turned, sems):
+def reduced_kernel(where_ref, flow, small_ref, out_ref, held, table, turned, sems):
     size = 1024 // BLOCKS
 
     def fetch(j):
@@ -34,13 +34,17 @@
 
     for j in range(BLOCKS):
         fetch(j).start()
-    wide = lax.broadcasted_iota(jnp.int32, (RZ, 128), 1) // RV == lax.broadcasted_iota(jnp.int32, (RZ, 128), 0)
-    z_wide = lax.dot_general(z_ref[...], wide.astype(jnp.bfloat16), TN, preferred_element_type=jnp.float32)
-    wide = lax.broadcasted_iota(jnp.int32, (RV, 128), 1) % RV == lax.broadcasted_iota(jnp.int32, (RV, 128), 0)
-    v_wide = lax.dot_general(v_ref[...], wide.astype(jnp.bfloat16), TN, preferred_element_type=jnp.float32)
+    wide = lax.broadcasted_iota(jnp.int32, (16, 128), 1) // RV == lax.broadcasted_iota(jnp.int32, (16, 128), 0)
+    z_wide = lax.dot_general(
+        small_ref[32:48, :], wide.astype(jnp.bfloat16), TN, preferred_element_type=jnp.float32
+    )
+    wide = lax.broadcasted_iota(jnp.int32, (16, 128), 1) % RV == lax.broadcasted_iota(jnp.int32, (16, 128), 0)
+    v_wide = lax.dot_general(
+        small_ref[48:64, :], wide.astype(jnp.bfloat16), TN, preferred_element_type=jnp.float32
+    )[:NV, :]
     for i in range(NZ):
         table[NV * i : NV * i + NV, :] = (z_wide[i : i + 1, :] * v_wide).astype(jnp.bfloat16)
-    half = y_ref[pl.ds(pl.multiple_of(where_ref[0] * 16, 16), 16), :].astype(jnp.float32)
+    half = small_ref[pl.ds(pl.multiple_of(where_ref[0] * 16, 16), 16), :].astype(jnp.float32)
     for p in range(32):
         out_ref[p * 48 + 32 : p * 48 + 48, :] = half
     for i in range(BLOCKS):
@@ -54,11 +58,19 @@
 
 
 def reduced_blocks(where, flow, y_factor, z_factor, v_factor):
+    small = jnp.concatenate(
+        [
+            y_factor,
+            jnp.pad(z_factor.T, ((0, 0), (0, 128 - NZ))),
+            jnp.pad(v_factor.T, ((0, 16 - RV), (0, 128 - NV))),
+        ],
+        axis=0,
+    )
     return pl.pallas_call(
         reduced_kernel,
         out_shape=jax.ShapeDtypeStruct((32 * 48, 128), jnp.float32),
         in_specs=[pl.BlockSpec(memory_space=pltpu.SMEM), pl.BlockSpec(memory_space=pl.ANY)]
-        + [pl.BlockSpec(memory_space=pltpu.VMEM)] * 3,
+        + [pl.BlockSpec(memory_space=pltpu.VMEM)],
         out_specs=pl.BlockSpec(memory_space=pltpu.VMEM),
         scratch_shapes=[
             pltpu.VMEM((BLOCKS, 1024 // BLOCKS, NZ * NV), jnp.bfloat16),
@@ -66,9 +78,9 @@
             pltpu.VMEM((128, 128), jnp.float32),
             pltpu.SemaphoreType.DMA((BLOCKS,)),
         ],
-        compiler_params=pltpu.CompilerParams(vmem_limit_bytes=56 * 1024 * 1024),
+        compiler_params=pltpu.CompilerParams(vmem_limit_bytes=53 * 1024 * 1024),
         name="reduced_blocks",
-    )(where, flow, y_factor, z_factor, v_factor)
+    )(where, flow, small)
 
 
 def projected_kernel(got, out_ref, own_ref, ordered):
@@ -191,22 +203,15 @@
     return jnp.concatenate(done, axis=0)
 
 
-def sweeps_kernel(where_ref, mine, other, rows_ref, cols_ref, parts, half, far, start, basis, sems):
-    z, h, c = where_ref[0], where_ref[1], where_ref[2]
-    first = pltpu.make_async_copy(mine, parts.at[c], sems.at[0])
-    second = pltpu.make_async_copy(other, parts.at[1 - c], sems.at[1])
-    first.start()
-    second.start()
-    first.wait()
-    second.wait()
+def assemble(parts, half, far, start, basis):
     lower_lanes = lax.broadcasted_iota(jnp.int32, (8, 128), 1) < 64
 
     for zz in range(16):
         for hh in range(2):
             for cc in range(2):
                 for e in range(2):
-                    start[pl.ds(zz * 64 + hh * 32 + 2 * cc + e, 8, stride=4), :] = parts[
-                        cc, pl.ds(hh * 8 * PART + 136 + 2 * zz + e, 8, stride=PART), :
+                    start[pl.ds(zz * 64 + hh * 32 + 2 * cc + e, 8, stride=4), :] = parts[cc][
+                        pl.ds(hh * 8 * PART + 136 + 2 * zz + e, 8, stride=PART), :
                     ]
     for zz in range(16):
         basis[:, zz * 64 : zz * 64 + 64] = start[zz * 64 : zz * 64 + 64, :].T
@@ -214,8 +219,8 @@
     for zz in range(8):
         for cc in range(2):
             for g in range(2):
-                far[pl.ds(zz * 32 + cc + 16 * g, 8, stride=2), :] = parts[
-                    cc, pl.ds(g * 8 * PART + 128 + zz, 8, stride=PART), :
+                far[pl.ds(zz * 32 + cc + 16 * g, 8, stride=2), :] = parts[cc][
+                    pl.ds(g * 8 * PART + 128 + zz, 8, stride=PART), :
                 ]
 
     def source(row_z, col_z, g):
@@ -224,7 +229,7 @@
         if d < 8:
             p = (d // 2) * 8 + g
             base = (p // 2) * PART + z_of * 8
-            return parts[p % 2, base : base + 8, :]
+            return parts[p % 2][base : base + 8, :]
         if d == 8 and z_of < 8:
             block = far[z_of * 32 + (g % 4) * 8 : z_of * 32 + (g % 4) * 8 + 8, :]
             if (g >= 4) != (col_z % 2 == 1):
@@ -248,6 +253,18 @@
             if i != j:
                 half[cols, rows] = block.T
 
+
+def sweeps_kernel(where_ref, mine, other, rows_ref, cols_ref, half, far, start, basis):
+    z, h, c = where_ref[0], where_ref[1], where_ref[2]
+
+    @pl.when(c == 0)
+    def _():
+        assemble((mine, other), half, far, start, basis)
+
+    @pl.when(c == 1)
+    def _():
+        assemble((other, mine), half, far, start, basis)
+
     def sweep(_, carry):
         image = dot(basis[...], half[...], NN)
         correlation = dot(image, image, NT)
@@ -286,17 +303,15 @@
         ),
         in_specs=[
             pl.BlockSpec(memory_space=pltpu.SMEM),
-            pl.BlockSpec(memory_space=pl.ANY),
-            pl.BlockSpec(memory_space=pl.ANY),
+            pl.BlockSpec(memory_space=pltpu.VMEM),
+            pl.BlockSpec(memory_space=pltpu.VMEM),
         ],
         out_specs=[pl.BlockSpec(memory_space=pltpu.VMEM)] * 2,
         scratch_shapes=[
-            pltpu.VMEM((2, 16 * PART, 128), jnp.float32),
             pltpu.VMEM((1024, 1024), jnp.float32),
             pltpu.VMEM((8 * 32, 128), jnp.float32),
             pltpu.VMEM((1024, 128), jnp.float32),
             pltpu.VMEM((128, 1024), jnp.float32),
-            pltpu.SemaphoreType.DMA((2,)),
         ],
         compiler_params=pltpu.CompilerParams(vmem_limit_bytes=32 * 1024 * 1024),
         name="sweeps",
@@ -308,7 +323,7 @@
     h = lax.axis_index("h").astype(jnp.int32)
     c = lax.axis_index("c").astype(jnp.int32)
     send = reduced_blocks(
-        h.reshape(1), flow_field.reshape(1024, NZ * NV), y_factor, z_factor.T, v_factor.T
+        h.reshape(1), flow_field.reshape(1024, NZ * NV), y_factor, z_factor, v_factor
     )
     got = lax.all_to_all(send.reshape(32, 48, 128), PLANE, 0, 0)
     projected, own = projected_rows(got.reshape(32 * 48, 128))

time: 195 us -> 193 us (0.990)
  no operation moved by 1% of the time
where the time goes in v5:
time: 193 us; the launch traced here: 192 us
  blocking collectives  75.3 us (39%)
  starting transfers between devices  41.5 us (22%)
  Pallas kernels  37.1 us (19%)
  waiting for transfers between devices  19 us (10%)
  between operations  14.2 us (7%)
  local copies, waits for them, and re-layouts  3.63 us (2%)
    pallas_call x1, Pallas kernels, sweeps(): pl.pallas_call(sweeps_kernel, out_shape=(jax.ShapeDtypeStruct((32, RX), j...  29.4 us
    ppermute x6, starting transfers between devices, from_z(): lax.ppermute(block, 'z', [(i, (i - distance) % 16) for i in range(16)])  25 us
    all_to_all x1, blocking collectives, local(): got = lax.all_to_all(send.reshape(32, 48, 128), PLANE, 0, 0)  23.6 us
    all_to_all x1, blocking collectives, local(): lax.all_to_all(jnp.broadcast_to(part[None], (16, 16, 128)), 'z', 0, 0)  21.7 us
    all_to_all x1, blocking collectives, local(): lax.all_to_all(jnp.broadcast_to(line[None], (16, PART, 128)), XY, 0, 0)  19.7 us
    all_to_all x1, blocking collectives, local(): core = lax.all_to_all(core, PLANE, 0, 0).reshape(32, 4, 4, 8)  10.2 us
    all_to_all x1, starting transfers between devices, local(): part = lax.all_to_all(strips(z, blocks), PLANE, 0, 0).sum(0)  9.97 us
    ppermute x6, waiting for transfers between devices, from_z(): lax.ppermute(block, 'z', [(i, (i - distance) % 16) for i in range(16)])  7.99 us
  transfers between devices with their start and end apart: 9, of which 5 were waited for; matrix products, arithmetic and copies ran while one was open for 0% of the time, Pallas kernels for 15%

profile of v5, /device:TPU:1, one launch (start us, length us, event | category | flops | bytes accessed | tf_op | source)
XLA Modules:
  0.0 191.8 jit_solution(17699472804589667612)
XLA Ops:
  7.2 0.0 copy-start
  7.2 0.7 fusion.4.small_ref
  7.9 3.4 %reduced_blocks.1 = f32[1536,128]{1,0:T(8,128)S(1)} custom-call(s32[1]{0:T(128)} %bitcast.1.where_ref, bf16[1024,2048]{1,0:T(8,128)(2,1)} %bitcast.28, bf16[64,128]{1,0:T(8,128)(2,1)S(1)} %fusion.4.small_ref), custom_call_target="tpu_custom_call" | custom-call | tf_op jit(solution)/shard_map/reduced_blocks/pallas_call | solution.py:69
  11.4 23.6 %all_to_all.25 = f32[32,48,128]{2,1,0:T(8,128)S(1)} all-to-all(f32[32,48,128]{2,1,0:T(8,128)S(1)} %bitcast.26), channel_id=1, replica_groups=mesh['z'=16,'h'=2,'y'=4,'l'=2,'c'=2] {'h','y','l','c'}, dimensions={0} | all-to-all | bytes 1572864 | tf_op jit(solution)/shard_map/all_to_all | solution.py:328
  35.0 1.1 projected_rows.1
  36.1 9.9 %collective-permute-start.3 = (f32[64,512]{1,0:T(8,128)S(1)}, f32[64,512]{1,0:T(8,128)S(1)}, u32[]{:S(2)}, u32[]{:S(2)}) collective-permute-start(f32[64,512]{1,0:T(8,128)S(1)} %get-tuple-element.7.refs_4_), channel_id=1, source_target_pairs={{0,480},{32,0},{64,32},{96,64},{128,96},{160,128},{192,160},{224,1... | collective-permute-start | bytes 393224 | tf_op jit(solution)/shard_map/ppermute | solution.py:332
  46.0 3.1 %collective-permute-start.4 = (f32[64,512]{1,0:T(8,128)S(1)}, f32[64,512]{1,0:T(8,128)S(1)}, u32[]{:S(2)}, u32[]{:S(2)}) collective-permute-start(f32[64,512]{1,0:T(8,128)S(1)} %get-tuple-element.7.refs_4_), channel_id=1, source_target_pairs={{0,448},{32,480},{64,0},{96,32},{128,64},{160,96},{192,128},{224,1... | collective-permute-start | bytes 393224 | tf_op jit(solution)/shard_map/ppermute | solution.py:332
  49.0 2.6 %collective-permute-start = (f32[64,512]{1,0:T(8,128)S(1)}, f32[64,512]{1,0:T(8,128)S(1)}, u32[]{:S(2)}, u32[]{:S(2)}) collective-permute-start(f32[64,512]{1,0:T(8,128)S(1)} %get-tuple-element.7.refs_4_), channel_id=1, source_target_pairs={{0,32},{32,64},{64,96},{96,128},{128,160},{160,192},{192,224},{224... | collective-permute-start | bytes 393224 | tf_op jit(solution)/shard_map/ppermute | solution.py:332
  51.7 2.4 %collective-permute-start.1 = (f32[64,512]{1,0:T(8,128)S(1)}, f32[64,512]{1,0:T(8,128)S(1)}, u32[]{:S(2)}, u32[]{:S(2)}) collective-permute-start(f32[64,512]{1,0:T(8,128)S(1)} %get-tuple-element.7.refs_4_), channel_id=1, source_target_pairs={{0,64},{32,96},{64,128},{96,160},{128,192},{160,224},{192,256},{22... | collective-permute-start | bytes 393224 | tf_op jit(solution)/shard_map/ppermute | solution.py:332
  54.1 0.0 collective-permute-done.3.refs_5_
  54.1 0.0 collective-permute-done.4.refs_6_
  54.1 5.0 %collective-permute-start.5 = (f32[128,512]{1,0:T(8,128)S(1)}, f32[128,512]{1,0:T(8,128)S(1)}, u32[]{:S(2)}, u32[]{:S(2)}) collective-permute-start(f32[128,512]{1,0:T(8,128)S(1)} %pad_maximum_fusion.1), channel_id=1, source_target_pairs={{0,448},{32,480},{64,0},{96,32},{128,64},{160,96},{192,128},{224,1... | collective-permute-start | bytes 786440 | tf_op jit(solution)/shard_map/ppermute | solution.py:332
  59.2 0.0 collective-permute-done.refs_3_
  59.2 0.8 collective-permute-done.1.refs_2_
  60.0 2.0 %collective-permute-start.2 = (f32[128,512]{1,0:T(8,128)S(1)}, f32[128,512]{1,0:T(8,128)S(1)}, u32[]{:S(2)}, u32[]{:S(2)}) collective-permute-start(f32[128,512]{1,0:T(8,128)S(1)} %pad_maximum_fusion), channel_id=1, source_target_pairs={{0,64},{32,96},{64,128},{96,160},{128,192},{160,224},{192,256},{22... | collective-permute-start | bytes 786440 | tf_op jit(solution)/shard_map/ppermute | solution.py:332
  62.1 6.8 %collective-permute-done.5 = f32[128,512]{1,0:T(8,128)S(1)} collective-permute-done((f32[128,512]{1,0:T(8,128)S(1)}, f32[128,512]{1,0:T(8,128)S(1)}, u32[]{:S(2)}, u32[]{:S(2)}) %collective-permute-start.5) | collective-permute-done | bytes 262176 | tf_op jit(solution)/shard_map/ppermute | solution.py:332
  68.9 0.4 collective-permute-done.2
  69.3 2.1 %strips.1 = f32[32,16,128]{2,1,0:T(8,128)} custom-call(s32[1]{0:T(128)} %bitcast.where_ref, f32[64,512]{1,0:T(8,128)S(1)} %get-tuple-element.15.refs_0_, f32[64,512]{1,0:T(8,128)S(1)} %get-tuple-element.14.refs_1_, f32[64,512]{1,0:T(8,128)S(1)} %collective-permute-done.1.refs_2_, f32[64,512]{1,0:T(8,128)S(1)} %collective-permute-done.refs_3_, ...), custom_call_target="tpu_custom_call" | custom-call | tf_op jit(solution)/shard_map/strips/pallas_call | solution.py:144
  71.4 10.0 %all-to-all-start.1 = ((f32[32,16,128]{2,1,0:T(8,128)}), f32[32,16,128]{2,1,0:T(8,128)S(1)}, u32[]{:S(2)}, u32[]{:S(2)}) async-start(f32[32,16,128]{2,1,0:T(8,128)} %strips.1), calls=%async_computation.1 | async-start | bytes 524288 | tf_op jit(solution)/shard_map/all_to_all | solution.py:344
  81.4 0.0 all-gather.3.cloned.1.call-start
  81.4 0.7 all-gather.3.cloned.1.call-update
  82.1 0.1 pad.15.clone
  82.2 0.0 copy-done
  82.2 7.7 %all-to-all-done.1 = f32[32,16,128]{2,1,0:T(8,128)S(1)} async-done(((f32[32,16,128]{2,1,0:T(8,128)}), f32[32,16,128]{2,1,0:T(8,128)S(1)}, u32[]{:S(2)}, u32[]{:S(2)}) %all-to-all-start.1) | async-done | bytes 262176 | tf_op jit(solution)/shard_map/all_to_all | solution.py:344
  90.0 0.1 maximum_maximum_fusion
  90.0 21.7 %all_to_all.26 = f32[16,16,128]{2,1,0:T(8,128)S(1)} all-to-all(f32[16,16,128]{2,1,0:T(8,128)S(1)} %broadcast_in_dim.7), channel_id=1, replica_groups=mesh['z'=16,'h'=2,'y'=4,'l'=2,'c'=2] {'z'}, dimensions={0} | all-to-all | bytes 262144 | tf_op jit(solution)/shard_map/all_to_all | solution.py:348
  111.8 0.1 broadcast_in_dim.8
  111.9 19.7 %all_to_all.27 = f32[16,168,128]{2,1,0:T(8,128)S(1)} all-to-all(f32[16,168,128]{2,1,0:T(8,128)S(1)} %broadcast_in_dim.8), channel_id=1, replica_groups=mesh['z'=16,'h'=2,'y'=4,'l'=2,'c'=2] {'h','y','l'}, dimensions={0} | all-to-all | bytes 2752512 | tf_op jit(solution)/shard_map/all_to_all | solution.py:352
  131.7 6.5 %collective-permute-start.6 = (f32[2688,128]{1,0:T(8,128)S(1)}, f32[2688,128]{1,0:T(8,128)S(1)}, u32[]{:S(2)}, u32[]{:S(2)}) collective-permute-start(f32[2688,128]{1,0:T(8,128)S(1)} %bitcast.24), channel_id=1, source_target_pairs={{0,1},{1,0},{2,3},{3,2},{4,5},{5,4},{6,7},{7,6},{8,9},{9,8},{10,11... | collective-permute-start | bytes 4128776 | tf_op jit(solution)/shard_map/ppermute | solution.py:354
  138.2 0.1 pad_add_fusion.where_ref
  138.3 2.7 %collective-permute-done.6.other = f32[2688,128]{1,0:T(8,128)S(1)} collective-permute-done((f32[2688,128]{1,0:T(8,128)S(1)}, f32[2688,128]{1,0:T(8,128)S(1)}, u32[]{:S(2)}, u32[]{:S(2)}) %collective-permute-start.6) | collective-permute-done | bytes 1376288 | tf_op jit(solution)/shard_map/ppermute | solution.py:354
  140.9 29.4 %sweeps.1 = (f32[32,128]{1,0:T(8,128)}, f32[8,1024]{1,0:T(8,128)S(1)}) custom-call(s32[3]{0:T(128)S(1)} %pad_add_fusion.where_ref, f32[2688,128]{1,0:T(8,128)S(1)} %bitcast.25, f32[2688,128]{1,0:T(8,128)S(1)} %collective-permute-done.6.other), custom_call_target="tpu_custom_call" | custom-call | tf_op jit(solution)/shard_map/sweeps/pallas_call | solution.py:298
  170.4 0.0 all-gather.3.cloned.1.call-done.every_ref
  170.4 0.0 copy-start.1
  170.4 1.6 copy-done.1
  172.0 1.0 core_rows.1
  173.0 0.2 reshape.48
  173.1 0.2 copy.13
  173.3 0.1 reshape.49
  173.4 0.1 copy.14
  173.5 10.2 %all_to_all.28 = f32[32,1,128]{2,1,0:T(1,128)S(1)} all-to-all(f32[32,1,128]{2,1,0:T(1,128)S(1)} %copy.14), channel_id=1, replica_groups=mesh['z'=16,'h'=2,'y'=4,'l'=2,'c'=2] {'h','y','l','c'}, dimensions={0} | all-to-all | bytes 32768 | tf_op jit(solution)/shard_map/all_to_all | solution.py:359
  183.7 0.1 copy.15
  183.8 0.3 copy.16
  184.0 0.9 reshape.51
  (12 shorter events, 0.2 us)
Async XLA Ops:
  7.2 75.0 %copy-start = (f32[32,128]{1,0:T(8,128)S(1)}, f32[32,128]{1,0:T(8,128)}, u32[]{:S(2)}) copy-start(f32[32,128]{1,0:T(8,128)} %param.9) | copy-start | bytes 49156
  36.1 18.0 %collective-permute-start.3 = (f32[64,512]{1,0:T(8,128)S(1)}, f32[64,512]{1,0:T(8,128)S(1)}, u32[]{:S(2)}, u32[]{:S(2)}) collective-permute-start(f32[64,512]{1,0:T(8,128)S(1)} %get-tuple-element.7.refs_4_), channel_id=1, source_target_pairs={{0,480},{32,0},{64,32},{96,64},{128,96},{160,128},{192,160},{224,1... | collective-permute-start | bytes 393224 | tf_op jit(solution)/shard_map/ppermute | solution.py:332
  46.0 8.1 %collective-permute-start.4 = (f32[64,512]{1,0:T(8,128)S(1)}, f32[64,512]{1,0:T(8,128)S(1)}, u32[]{:S(2)}, u32[]{:S(2)}) collective-permute-start(f32[64,512]{1,0:T(8,128)S(1)} %get-tuple-element.7.refs_4_), channel_id=1, source_target_pairs={{0,448},{32,480},{64,0},{96,32},{128,64},{160,96},{192,128},{224,1... | collective-permute-start | bytes 393224 | tf_op jit(solution)/shard_map/ppermute | solution.py:332
  49.0 10.1 %collective-permute-start = (f32[64,512]{1,0:T(8,128)S(1)}, f32[64,512]{1,0:T(8,128)S(1)}, u32[]{:S(2)}, u32[]{:S(2)}) collective-permute-start(f32[64,512]{1,0:T(8,128)S(1)} %get-tuple-element.7.refs_4_), channel_id=1, source_target_pairs={{0,32},{32,64},{64,96},{96,128},{128,160},{160,192},{192,224},{224... | collective-permute-start | bytes 393224 | tf_op jit(solution)/shard_map/ppermute | solution.py:332
  51.7 8.3 %collective-permute-start.1 = (f32[64,512]{1,0:T(8,128)S(1)}, f32[64,512]{1,0:T(8,128)S(1)}, u32[]{:S(2)}, u32[]{:S(2)}) collective-permute-start(f32[64,512]{1,0:T(8,128)S(1)} %get-tuple-element.7.refs_4_), channel_id=1, source_target_pairs={{0,64},{32,96},{64,128},{96,160},{128,192},{160,224},{192,256},{22... | collective-permute-start | bytes 393224 | tf_op jit(solution)/shard_map/ppermute | solution.py:332
  54.1 14.7 %collective-permute-start.5 = (f32[128,512]{1,0:T(8,128)S(1)}, f32[128,512]{1,0:T(8,128)S(1)}, u32[]{:S(2)}, u32[]{:S(2)}) collective-permute-start(f32[128,512]{1,0:T(8,128)S(1)} %pad_maximum_fusion.1), channel_id=1, source_target_pairs={{0,448},{32,480},{64,0},{96,32},{128,64},{160,96},{192,128},{224,1... | collective-permute-start | bytes 786440 | tf_op jit(solution)/shard_map/ppermute | solution.py:332
  60.0 9.3 %collective-permute-start.2 = (f32[128,512]{1,0:T(8,128)S(1)}, f32[128,512]{1,0:T(8,128)S(1)}, u32[]{:S(2)}, u32[]{:S(2)}) collective-permute-start(f32[128,512]{1,0:T(8,128)S(1)} %pad_maximum_fusion), channel_id=1, source_target_pairs={{0,64},{32,96},{64,128},{96,160},{128,192},{160,224},{192,256},{22... | collective-permute-start | bytes 786440 | tf_op jit(solution)/shard_map/ppermute | solution.py:332
  71.4 18.5 %all-to-all-start.1 = ((f32[32,16,128]{2,1,0:T(8,128)}), f32[32,16,128]{2,1,0:T(8,128)S(1)}, u32[]{:S(2)}, u32[]{:S(2)}) async-start(f32[32,16,128]{2,1,0:T(8,128)} %strips.1), calls=%async_computation.1 | async-start | bytes 524288 | tf_op jit(solution)/shard_map/all_to_all | solution.py:344
  81.4 89.0 %all-gather.3.cloned.1.call-start = ((), (), s32[]{:S(2)}) async-start(), calls=%async_computation.5 | async-start | bytes 2228224 | tf_op jit(solution)/shard_map/all_gather | solution.py:342
  131.7 9.3 %collective-permute-start.6 = (f32[2688,128]{1,0:T(8,128)S(1)}, f32[2688,128]{1,0:T(8,128)S(1)}, u32[]{:S(2)}, u32[]{:S(2)}) collective-permute-start(f32[2688,128]{1,0:T(8,128)S(1)} %bitcast.24), channel_id=1, source_target_pairs={{0,1},{1,0},{2,3},{3,2},{4,5},{5,4},{6,7},{7,6},{8,9},{9,8},{10,11... | collective-permute-start | bytes 4128776 | tf_op jit(solution)/shard_map/ppermute | solution.py:354
  170.4 1.6 copy-start.1
Sparse Core Ops, SparseCore 0:
  84.3 68.2 all-gather.2

commit v6 on v5

--- a/solution.py
+++ b/solution.py
@@ -272,26 +272,9 @@
         return carry
 
     lax.fori_loop(0, ITERS, sweep, 0)
-    pick = lax.broadcasted_iota(jnp.int32, (32, 1024), 1) == (
-        lax.broadcasted_iota(jnp.int32, (32, 1024), 0) + (z * 2 + h) * 32
-    )
-    rows_ref[...] = dot(jnp.where(pick, 1.0, 0.0), basis[...], NT)
+    ahead = pltpu.roll(basis[...], lax.rem((32 - (z * 2 + h)) * 32, 1024), 1)
+    rows_ref[...] = ahead[:, :128].T[:32, :]
     cols_ref[...] = basis[pl.ds(pl.multiple_of(z * 8, 8), 8), :]
-
-
-def core_kernel(cols_ref, every_ref, core_ref):
-    core_ref[...] = dot(cols_ref[...], every_ref[...], NN)
-
-
-def core_rows(cols, every):
-    return pl.pallas_call(
-        core_kernel,
-        out_shape=jax.ShapeDtypeStruct((8, 512), jnp.float32),
-        in_specs=[pl.BlockSpec(memory_space=pltpu.VMEM)] * 2,
-        out_specs=pl.BlockSpec(memory_space=pltpu.VMEM),
-        compiler_params=pltpu.CompilerParams(vmem_limit_bytes=16 * 1024 * 1024),
-        name="core_rows",
-    )(cols, every)
 
 
 def sweeps(where, mine, other):
@@ -354,7 +337,7 @@
     other = lax.ppermute(mine, "c", [(0, 1), (1, 0)])
 
     x_factor, cols = sweeps(jnp.stack([z, h, c]), mine, other)
-    core = core_rows(cols, every)
+    core = dot(cols, every, NN)
     core = core.reshape(2, 4, 4, 16, 8).transpose(0, 3, 1, 2, 4).reshape(32, 1, 128)
     core = lax.all_to_all(core, PLANE, 0, 0).reshape(32, 4, 4, 8)
     core = core.transpose(1, 3, 0, 2).reshape(4, 1024)

time: 193 us -> 200 us (1.036)
  matrix products: 0 us -> 7.85 us
    dot_general x0 -> x1, matrix products: none -> 7.85 us  [dot(): lax.dot_general(a, b, dims, precision=HIGHEST, preferred_element_type=jnp...]
    dot_general x0 -> x2, local copies, waits for them, and re-layouts: none -> 2.16 us  [dot(): lax.dot_general(a, b, dims, precision=HIGHEST, preferred_element_type=jnp...]
where the time goes in v6:
time: 200 us; the launch traced here: 199 us
  blocking collectives  75.2 us (38%)
  starting transfers between devices  41.6 us (21%)
  Pallas kernels  35.7 us (18%)
  waiting for transfers between devices  19 us (10%)
  between operations  14.3 us (7%)
  matrix products  7.85 us (4%)
  local copies, waits for them, and re-layouts  3.98 us (2%)
    pallas_call x1, Pallas kernels, sweeps(): pl.pallas_call(sweeps_kernel, out_shape=(jax.ShapeDtypeStruct((32, RX), j...  29.1 us
    ppermute x6, starting transfers between devices, from_z(): lax.ppermute(block, 'z', [(i, (i - distance) % 16) for i in range(16)])  25 us
    all_to_all x1, blocking collectives, local(): got = lax.all_to_all(send.reshape(32, 48, 128), PLANE, 0, 0)  23.6 us
    all_to_all x1, blocking collectives, local(): lax.all_to_all(jnp.broadcast_to(part[None], (16, 16, 128)), 'z', 0, 0)  21.7 us
    all_to_all x1, blocking collectives, local(): lax.all_to_all(jnp.broadcast_to(line[None], (16, PART, 128)), XY, 0, 0)  19.7 us
    all_to_all x1, blocking collectives, local(): core = lax.all_to_all(core, PLANE, 0, 0).reshape(32, 4, 4, 8)  10.2 us
    all_to_all x1, starting transfers between devices, local(): part = lax.all_to_all(strips(z, blocks), PLANE, 0, 0).sum(0)  10 us
    ppermute x6, waiting for transfers between devices, from_z(): lax.ppermute(block, 'z', [(i, (i - distance) % 16) for i in range(16)])  7.96 us
  transfers between devices with their start and end apart: 9, of which 5 were waited for; matrix products, arithmetic and copies ran while one was open for 0% of the time, Pallas kernels for 15%

profile of v6, /device:TPU:1, one launch (start us, length us, event | category | flops | bytes accessed | tf_op | source)
XLA Modules:
  0.0 198.6 jit_solution(18320599243656973279)
XLA Ops:
  7.2 0.0 copy-start
  7.2 0.7 fusion.11.small_ref
  7.9 3.4 %reduced_blocks.1 = f32[1536,128]{1,0:T(8,128)S(1)} custom-call(s32[1]{0:T(128)} %bitcast.1.where_ref, bf16[1024,2048]{1,0:T(8,128)(2,1)} %bitcast.40, bf16[64,128]{1,0:T(8,128)(2,1)S(1)} %fusion.11.small_ref), custom_call_target="tpu_custom_call" | custom-call | tf_op jit(solution)/shard_map/reduced_blocks/pallas_call | solution.py:69
  11.4 23.6 %all_to_all.25 = f32[32,48,128]{2,1,0:T(8,128)S(1)} all-to-all(f32[32,48,128]{2,1,0:T(8,128)S(1)} %bitcast.37), channel_id=1, replica_groups=mesh['z'=16,'h'=2,'y'=4,'l'=2,'c'=2] {'h','y','l','c'}, dimensions={0} | all-to-all | bytes 1572864 | tf_op jit(solution)/shard_map/all_to_all | solution.py:311
  35.0 1.1 projected_rows.1
  36.1 9.9 %collective-permute-start.3 = (f32[64,512]{1,0:T(8,128)S(1)}, f32[64,512]{1,0:T(8,128)S(1)}, u32[]{:S(2)}, u32[]{:S(2)}) collective-permute-start(f32[64,512]{1,0:T(8,128)S(1)} %get-tuple-element.7.refs_4_), channel_id=1, source_target_pairs={{0,480},{32,0},{64,32},{96,64},{128,96},{160,128},{192,160},{224,1... | collective-permute-start | bytes 393224 | tf_op jit(solution)/shard_map/ppermute | solution.py:315
  46.0 3.1 %collective-permute-start.4 = (f32[64,512]{1,0:T(8,128)S(1)}, f32[64,512]{1,0:T(8,128)S(1)}, u32[]{:S(2)}, u32[]{:S(2)}) collective-permute-start(f32[64,512]{1,0:T(8,128)S(1)} %get-tuple-element.7.refs_4_), channel_id=1, source_target_pairs={{0,448},{32,480},{64,0},{96,32},{128,64},{160,96},{192,128},{224,1... | collective-permute-start | bytes 393224 | tf_op jit(solution)/shard_map/ppermute | solution.py:315
  49.0 2.6 %collective-permute-start = (f32[64,512]{1,0:T(8,128)S(1)}, f32[64,512]{1,0:T(8,128)S(1)}, u32[]{:S(2)}, u32[]{:S(2)}) collective-permute-start(f32[64,512]{1,0:T(8,128)S(1)} %get-tuple-element.7.refs_4_), channel_id=1, source_target_pairs={{0,32},{32,64},{64,96},{96,128},{128,160},{160,192},{192,224},{224... | collective-permute-start | bytes 393224 | tf_op jit(solution)/shard_map/ppermute | solution.py:315
  51.7 2.4 %collective-permute-start.1 = (f32[64,512]{1,0:T(8,128)S(1)}, f32[64,512]{1,0:T(8,128)S(1)}, u32[]{:S(2)}, u32[]{:S(2)}) collective-permute-start(f32[64,512]{1,0:T(8,128)S(1)} %get-tuple-element.7.refs_4_), channel_id=1, source_target_pairs={{0,64},{32,96},{64,128},{96,160},{128,192},{160,224},{192,256},{22... | collective-permute-start | bytes 393224 | tf_op jit(solution)/shard_map/ppermute | solution.py:315
  54.1 0.0 collective-permute-done.3.refs_5_
  54.1 0.0 collective-permute-done.4.refs_6_
  54.1 5.0 %collective-permute-start.5 = (f32[128,512]{1,0:T(8,128)S(1)}, f32[128,512]{1,0:T(8,128)S(1)}, u32[]{:S(2)}, u32[]{:S(2)}) collective-permute-start(f32[128,512]{1,0:T(8,128)S(1)} %pad_maximum_fusion.1), channel_id=1, source_target_pairs={{0,448},{32,480},{64,0},{96,32},{128,64},{160,96},{192,128},{224,1... | collective-permute-start | bytes 786440 | tf_op jit(solution)/shard_map/ppermute | solution.py:315
  59.2 0.0 collective-permute-done.refs_3_
  59.2 0.8 collective-permute-done.1.refs_2_
  60.0 2.1 %collective-permute-start.2 = (f32[128,512]{1,0:T(8,128)S(1)}, f32[128,512]{1,0:T(8,128)S(1)}, u32[]{:S(2)}, u32[]{:S(2)}) collective-permute-start(f32[128,512]{1,0:T(8,128)S(1)} %pad_maximum_fusion), channel_id=1, source_target_pairs={{0,64},{32,96},{64,128},{96,160},{128,192},{160,224},{192,256},{22... | collective-permute-start | bytes 786440 | tf_op jit(solution)/shard_map/ppermute | solution.py:315
  62.1 6.8 %collective-permute-done.5 = f32[128,512]{1,0:T(8,128)S(1)} collective-permute-done((f32[128,512]{1,0:T(8,128)S(1)}, f32[128,512]{1,0:T(8,128)S(1)}, u32[]{:S(2)}, u32[]{:S(2)}) %collective-permute-start.5) | collective-permute-done | bytes 262176 | tf_op jit(solution)/shard_map/ppermute | solution.py:315
  68.9 0.3 collective-permute-done.2
  69.3 2.1 %strips.1 = f32[32,16,128]{2,1,0:T(8,128)} custom-call(s32[1]{0:T(128)} %bitcast.where_ref, f32[64,512]{1,0:T(8,128)S(1)} %get-tuple-element.15.refs_0_, f32[64,512]{1,0:T(8,128)S(1)} %get-tuple-element.14.refs_1_, f32[64,512]{1,0:T(8,128)S(1)} %collective-permute-done.1.refs_2_, f32[64,512]{1,0:T(8,128)S(1)} %collective-permute-done.refs_3_, ...), custom_call_target="tpu_custom_call" | custom-call | tf_op jit(solution)/shard_map/strips/pallas_call | solution.py:144
  71.4 10.0 %all-to-all-start.1 = ((f32[32,16,128]{2,1,0:T(8,128)}), f32[32,16,128]{2,1,0:T(8,128)S(1)}, u32[]{:S(2)}, u32[]{:S(2)}) async-start(f32[32,16,128]{2,1,0:T(8,128)} %strips.1), calls=%async_computation.1 | async-start | bytes 524288 | tf_op jit(solution)/shard_map/all_to_all | solution.py:327
  81.4 0.0 all-gather.3.cloned.1.call-start
  81.5 0.7 all-gather.3.cloned.1.call-update
  82.2 0.1 pad.15.clone
  82.2 0.0 copy-done
  82.3 7.7 %all-to-all-done.1 = f32[32,16,128]{2,1,0:T(8,128)S(1)} async-done(((f32[32,16,128]{2,1,0:T(8,128)}), f32[32,16,128]{2,1,0:T(8,128)S(1)}, u32[]{:S(2)}, u32[]{:S(2)}) %all-to-all-start.1) | async-done | bytes 262176 | tf_op jit(solution)/shard_map/all_to_all | solution.py:327
  90.0 0.1 maximum_maximum_fusion
  90.1 21.7 %all_to_all.26 = f32[16,16,128]{2,1,0:T(8,128)S(1)} all-to-all(f32[16,16,128]{2,1,0:T(8,128)S(1)} %broadcast_in_dim.7), channel_id=1, replica_groups=mesh['z'=16,'h'=2,'y'=4,'l'=2,'c'=2] {'z'}, dimensions={0} | all-to-all | bytes 262144 | tf_op jit(solution)/shard_map/all_to_all | solution.py:331
  111.8 0.1 broadcast_in_dim.8
  111.9 19.7 %all_to_all.27 = f32[16,168,128]{2,1,0:T(8,128)S(1)} all-to-all(f32[16,168,128]{2,1,0:T(8,128)S(1)} %broadcast_in_dim.8), channel_id=1, replica_groups=mesh['z'=16,'h'=2,'y'=4,'l'=2,'c'=2] {'h','y','l'}, dimensions={0} | all-to-all | bytes 2752512 | tf_op jit(solution)/shard_map/all_to_all | solution.py:335
  131.7 6.5 %collective-permute-start.6 = (f32[2688,128]{1,0:T(8,128)S(1)}, f32[2688,128]{1,0:T(8,128)S(1)}, u32[]{:S(2)}, u32[]{:S(2)}) collective-permute-start(f32[2688,128]{1,0:T(8,128)S(1)} %bitcast.35), channel_id=1, source_target_pairs={{0,1},{1,0},{2,3},{3,2},{4,5},{5,4},{6,7},{7,6},{8,9},{9,8},{10,11... | collective-permute-start | bytes 4128776 | tf_op jit(solution)/shard_map/ppermute | solution.py:337
  138.2 0.1 pad_add_fusion.where_ref
  138.3 2.7 %collective-permute-done.6.other = f32[2688,128]{1,0:T(8,128)S(1)} collective-permute-done((f32[2688,128]{1,0:T(8,128)S(1)}, f32[2688,128]{1,0:T(8,128)S(1)}, u32[]{:S(2)}, u32[]{:S(2)}) %collective-permute-start.6) | collective-permute-done | bytes 1376288 | tf_op jit(solution)/shard_map/ppermute | solution.py:337
  140.9 29.1 %sweeps.1 = (f32[32,128]{1,0:T(8,128)}, f32[8,1024]{1,0:T(8,128)S(1)}) custom-call(s32[3]{0:T(128)S(1)} %pad_add_fusion.where_ref, f32[2688,128]{1,0:T(8,128)S(1)} %bitcast.36, f32[2688,128]{1,0:T(8,128)S(1)} %collective-permute-done.6.other), custom_call_target="tpu_custom_call" | custom-call | tf_op jit(solution)/shard_map/sweeps/pallas_call | solution.py:281
  170.0 0.0 all-gather.3.cloned.1.call-done
  170.1 2.1 %copy.16 = f32[512,1024]{1,0:T(8,128)S(1)} copy(f32[512,1024]{0,1:T(8,128)} %bitcast.41) | data formatting | bytes 4194304 | tf_op jit(solution)/shard_map/dot_general | solution.py:26
  172.2 7.8 %fusion.3 = f32[2,16,4,4,8]{1,2,4,3,0:T(4,128)S(1)} fusion(f32[4,16,8,1024]{3,2,1,0:T(8,128)S(1)} %bitcast.39, f32[2,4,1024,1,1]{2,1,0,3,4:T(4,128)S(1)} %reshape.53), kind=kOutput, calls=%fused_computation.3 | convolution fusion | flops 50331648 | bytes 2146304 | tf_op jit(solution)/shard_map/dot_general | solution.py:26
  180.1 0.1 copy.18
  180.2 0.1 reshape.48
  180.3 0.1 copy.19
  180.4 10.2 %all_to_all.28 = f32[32,1,128]{2,1,0:T(1,128)S(1)} all-to-all(f32[32,1,128]{2,1,0:T(1,128)S(1)} %copy.19), channel_id=1, replica_groups=mesh['z'=16,'h'=2,'y'=4,'l'=2,'c'=2] {'h','y','l','c'}, dimensions={0} | all-to-all | bytes 32768 | tf_op jit(solution)/shard_map/all_to_all | solution.py:342
  190.5 0.1 copy.20
  190.6 0.3 copy.21
  190.9 0.9 reshape.50
  (13 shorter events, 0.2 us)
Async XLA Ops:
  7.2 75.1 %copy-start = (f32[32,128]{1,0:T(8,128)S(1)}, f32[32,128]{1,0:T(8,128)}, u32[]{:S(2)}) copy-start(f32[32,128]{1,0:T(8,128)} %param.9) | copy-start | bytes 49156
  36.1 18.0 %collective-permute-start.3 = (f32[64,512]{1,0:T(8,128)S(1)}, f32[64,512]{1,0:T(8,128)S(1)}, u32[]{:S(2)}, u32[]{:S(2)}) collective-permute-start(f32[64,512]{1,0:T(8,128)S(1)} %get-tuple-element.7.refs_4_), channel_id=1, source_target_pairs={{0,480},{32,0},{64,32},{96,64},{128,96},{160,128},{192,160},{224,1... | collective-permute-start | bytes 393224 | tf_op jit(solution)/shard_map/ppermute | solution.py:315
  46.0 8.1 %collective-permute-start.4 = (f32[64,512]{1,0:T(8,128)S(1)}, f32[64,512]{1,0:T(8,128)S(1)}, u32[]{:S(2)}, u32[]{:S(2)}) collective-permute-start(f32[64,512]{1,0:T(8,128)S(1)} %get-tuple-element.7.refs_4_), channel_id=1, source_target_pairs={{0,448},{32,480},{64,0},{96,32},{128,64},{160,96},{192,128},{224,1... | collective-permute-start | bytes 393224 | tf_op jit(solution)/shard_map/ppermute | solution.py:315
  49.0 10.1 %collective-permute-start = (f32[64,512]{1,0:T(8,128)S(1)}, f32[64,512]{1,0:T(8,128)S(1)}, u32[]{:S(2)}, u32[]{:S(2)}) collective-permute-start(f32[64,512]{1,0:T(8,128)S(1)} %get-tuple-element.7.refs_4_), channel_id=1, source_target_pairs={{0,32},{32,64},{64,96},{96,128},{128,160},{160,192},{192,224},{224... | collective-permute-start | bytes 393224 | tf_op jit(solution)/shard_map/ppermute | solution.py:315
  51.7 8.3 %collective-permute-start.1 = (f32[64,512]{1,0:T(8,128)S(1)}, f32[64,512]{1,0:T(8,128)S(1)}, u32[]{:S(2)}, u32[]{:S(2)}) collective-permute-start(f32[64,512]{1,0:T(8,128)S(1)} %get-tuple-element.7.refs_4_), channel_id=1, source_target_pairs={{0,64},{32,96},{64,128},{96,160},{128,192},{160,224},{192,256},{22... | collective-permute-start | bytes 393224 | tf_op jit(solution)/shard_map/ppermute | solution.py:315
  54.1 14.7 %collective-permute-start.5 = (f32[128,512]{1,0:T(8,128)S(1)}, f32[128,512]{1,0:T(8,128)S(1)}, u32[]{:S(2)}, u32[]{:S(2)}) collective-permute-start(f32[128,512]{1,0:T(8,128)S(1)} %pad_maximum_fusion.1), channel_id=1, source_target_pairs={{0,448},{32,480},{64,0},{96,32},{128,64},{160,96},{192,128},{224,1... | collective-permute-start | bytes 786440 | tf_op jit(solution)/shard_map/ppermute | solution.py:315
  60.0 9.2 %collective-permute-start.2 = (f32[128,512]{1,0:T(8,128)S(1)}, f32[128,512]{1,0:T(8,128)S(1)}, u32[]{:S(2)}, u32[]{:S(2)}) collective-permute-start(f32[128,512]{1,0:T(8,128)S(1)} %pad_maximum_fusion), channel_id=1, source_target_pairs={{0,64},{32,96},{64,128},{96,160},{128,192},{160,224},{192,256},{22... | collective-permute-start | bytes 786440 | tf_op jit(solution)/shard_map/ppermute | solution.py:315
  71.4 18.6 %all-to-all-start.1 = ((f32[32,16,128]{2,1,0:T(8,128)}), f32[32,16,128]{2,1,0:T(8,128)S(1)}, u32[]{:S(2)}, u32[]{:S(2)}) async-start(f32[32,16,128]{2,1,0:T(8,128)} %strips.1), calls=%async_computation.1 | async-start | bytes 524288 | tf_op jit(solution)/shard_map/all_to_all | solution.py:327
  81.4 88.6 %all-gather.3.cloned.1.call-start = ((), (), s32[]{:S(2)}) async-start(), calls=%async_computation.5 | async-start | bytes 2228224 | tf_op jit(solution)/shard_map/all_gather | solution.py:325
  131.7 9.3 %collective-permute-start.6 = (f32[2688,128]{1,0:T(8,128)S(1)}, f32[2688,128]{1,0:T(8,128)S(1)}, u32[]{:S(2)}, u32[]{:S(2)}) collective-permute-start(f32[2688,128]{1,0:T(8,128)S(1)} %bitcast.35), channel_id=1, source_target_pairs={{0,1},{1,0},{2,3},{3,2},{4,5},{5,4},{6,7},{7,6},{8,9},{9,8},{10,11... | collective-permute-start | bytes 4128776 | tf_op jit(solution)/shard_map/ppermute | solution.py:337
Sparse Core Ops, SparseCore 0:
  84.3 68.2 all-gather.2
